TPU v7x, 128 devices: a whole 4x4x4 slice. The times are simulated.
128 devices in a mesh: pair: 32 (over x, y, core), grid: 4 (over z).
Axes of the slice: x: 4, y: 4, z: 4, core: 2. Of those that a mesh axis runs over, the one named last changes fastest.
Arguments:
- b_tiles: float32 [8192, 128, 128], P(('pair', 'grid')), may hold values from -0.6 to 0.6
- tile_aux: int32 [8192], P(('pair', 'grid')), may hold values from 0 to 19, as said below
- tile_pair: int32 [8192], P(('pair', 'grid')), may hold values from 0 to 1535, as said below
- freq_weights: float32 [2, 196608], P(None, ('pair', 'grid')), may hold values from 0.1 to 2
- kept: int32 [128, 2], replicated, may hold values from 0 to 19, as said below
Outputs:
- pi_tiles: float32 [128, 2, 128, 128], P(('pair', 'grid'))
Inputs may be any that keep to these rules, and one draw needn't show every extreme that they name: `tile_aux`: never falling along the list. `tile_pair`: pair block b belongs to the device at index b // 12 of pair+grid. Of the tiles on one device at most 2 belong to one device's pair blocks, and in every draw some device receives exactly 2 tiles from every device. `kept`: each row (P, Q) has P < Q, and no two rows are equal.
All inputs are finite; a program needn't handle non-finite values.
Results may differ from a plain program's by a relative error of at most 0.00012.
Values sent between devices are 32-bit elements; how exact they have to be, the bound alone decides.
No kernel may reach another device: no remote copies, remote signals or barrier semaphores. Data moves between devices by JAX's collectives and lax.ppermute only.
A program may use at most 256 MiB of HBM per device.

v0:
```python
import math

import jax
import jax.numpy as jnp
from jax import lax
from jax.sharding import PartitionSpec as P

NAB = 20
CAP = 2


def tile_block(picked, dense_own, weights):
    left_rows = dense_own[picked[:, 0]]
    right_rows = dense_own[picked[:, 1]]
    scaled = left_rows[:, None] * weights[None, :, :, None, :]
    return jnp.einsum(
        "bfnik,bnjk->bfij",
        scaled,
        right_rows,
        precision=lax.Precision.HIGHEST,
        preferred_element_type=jnp.float32,
    )


def tile_terms(tile_picks, dense_own, weights):
    row_count = tile_picks.shape[0]
    block_size = math.gcd(row_count, 8)
    grouped = tile_picks.reshape(row_count // block_size, block_size, 2)
    partials = lax.map(lambda picked: tile_block(picked, dense_own, weights), grouped)
    return partials.reshape((row_count,) + partials.shape[2:])


def on_device(b_tiles, tile_aux, tile_pair, freq_weights, kept):
    devices = lax.axis_size(("pair", "grid"))
    tile_width = b_tiles.shape[1]
    local_blocks = freq_weights.shape[1] // tile_width
    owner_index = tile_pair // local_blocks
    matches = (owner_index[:, None] == jnp.arange(devices, dtype=jnp.int32)[None, :]).astype(
        jnp.int32
    )
    slot_rank = jnp.sum(jnp.cumsum(matches, axis=0) * matches, axis=1) - 1
    slot_index = owner_index * CAP + slot_rank
    slot_target = tile_aux * local_blocks + tile_pair % local_blocks
    send_tiles = (
        jnp.zeros((devices * CAP, tile_width, tile_width), jnp.float32).at[slot_index].set(b_tiles)
    )
    send_target = (
        jnp.full((devices * CAP,), NAB * local_blocks, jnp.int32).at[slot_index].set(slot_target)
    )
    received, got_target = (
        lax.all_to_all(
            send_tiles.reshape(devices, CAP, tile_width, tile_width),
            ("pair", "grid"),
            split_axis=0,
            concat_axis=0,
            tiled=True,
        ),
        lax.all_to_all(
            send_target.reshape(devices, CAP),
            ("pair", "grid"),
            split_axis=0,
            concat_axis=0,
            tiled=True,
        ),
    )
    dense_flat = jnp.zeros((NAB * local_blocks + 1, tile_width, tile_width), jnp.float32)
    dense_flat = dense_flat.at[got_target.reshape(-1)].add(
        received.reshape(-1, tile_width, tile_width)
    )
    dense_own = dense_flat[:-1].reshape(NAB, local_blocks, tile_width, tile_width)
    weights = freq_weights.reshape(2, local_blocks, tile_width)
    return lax.psum_scatter(
        tile_terms(kept, dense_own, weights), ("pair", "grid"), scatter_dimension=0, tiled=True
    )


def solution(mesh):
    placed = (
        P(("pair", "grid"), None, None),
        P(("pair", "grid")),
        P(("pair", "grid")),
        P(None, ("pair", "grid")),
        P(),
    )
    return jax.shard_map(
        on_device,
        mesh=mesh,
        in_specs=placed,
        out_specs=P(("pair", "grid"), None, None, None),
        check_vma=False,
    )
```

profile of v0, /device:TPU:1, one launch (start us, length us, event | category | flops | bytes accessed | tf_op | source)
XLA Modules:
  0.0 1553.9 jit_solution(8257351711866064969)
XLA Ops:
  9.1 11.5 all-to-all-start
  28.5 11.9 scatter_fusion
  40.4 10.2 all-to-all-start.1
  52.5 221.9 %all-to-all-done.1 = f32[128,2,128,128]{3,2,1,0:T(8,128)} async-done(((f32[128,2,128,128]{3,2,1,0:T(8,128)}), f32[128,2,128,128]{3,2,1,0:T(8,128)}, u32[]{:S(2)}, u32[]{:S(2)}) %all-to-all-start.1) | async-done | bytes 16777248 | tf_op jit(solution)/shard_map/all_to_all | solution.py:51
  281.9 52.8 %scatter_fusion.1 = f32[241,128,128]{2,1,0:T(8,128)} fusion(f32[241,128,128]{2,1,0:T(8,128)} %broadcast_in_dim.27, s32[256]{0:T(256)S(1)} %bitcast.42, f32[256,128,128]{2,1,0:T(8,128)} %bitcast.11), kind=kCustom, calls=%fused_computation.4 | custom fusion | flops 4194304 | bytes 50332672 | tf_op jit(solution)/shard_map/scatter-add | solution.py:67
  334.7 14.0 slice.14
  348.7 535.4 %while.10 = (s32[]{:T(128)}, f32[16,8,2,128,128]{4,3,2,1,0:T(8,128)}, s32[16,8,2]{1,0,2:T(8,128)S(1)}, f32[20,12,128,128]{3,2,1,0:T(8,128)}, f32[2,1536]{1,0:T(2,128)S(1)}, /*index=5*/s32[]{:T(128)}) while((s32[]{:T(128)}, f32[16,8,2,128,128]{4,3,2,1,0:T(8,128)}, s32[16,8,2]{1,0,2:T(8,128)S(1)}, f32[20,12,128,128]{3,2,1,0:T(8,128)}, ...), condition=%wide.region_6.7_spmd, body=%wide.region_5.6_spmd.sunk | while | flops 4834985984 | bytes 38843336 | solution.py:29
  348.7 9.2 gather_fusion
  357.9 9.0 gather_fusion.1
  366.9 15.2 fusion.28
  382.2 9.2 gather_fusion
  391.3 9.0 gather_fusion.1
  400.4 15.2 fusion.28
  415.7 9.2 gather_fusion
  424.8 9.0 gather_fusion.1
  433.8 15.2 fusion.28
  449.1 9.2 gather_fusion
  458.3 9.0 gather_fusion.1
  467.3 15.2 fusion.28
  482.6 9.2 gather_fusion
  491.7 9.0 gather_fusion.1
  500.8 15.2 fusion.28
  516.0 9.2 gather_fusion
  525.2 9.0 gather_fusion.1
  534.2 15.2 fusion.28
  549.5 9.2 gather_fusion
  558.7 9.0 gather_fusion.1
  567.7 15.3 fusion.28
  583.0 9.2 gather_fusion
  592.1 9.0 gather_fusion.1
  601.2 15.2 fusion.28
  616.4 9.2 gather_fusion
  634.6 15.3 fusion.28
  649.9 9.2 gather_fusion
  668.1 15.2 fusion.28
  683.4 9.2 gather_fusion
  701.6 15.2 fusion.28
  716.8 9.2 gather_fusion
  735.0 15.2 fusion.28
  750.3 9.2 gather_fusion
  768.5 15.3 fusion.28
  783.8 9.2 gather_fusion
  802.0 15.2 fusion.28
  817.2 9.2 gather_fusion
  835.4 15.2 fusion.28
  850.7 9.2 gather_fusion
  868.9 15.2 fusion.28
  884.1 662.9 %reduce-scatter.2.cloned.1.call-done = f32[1,2,128,128]{3,2,1,0:T(8,128)} async-done(((f32[128,2,128,128]{3,2,1,0:T(8,128)}), f32[1,2,128,128]{3,2,1,0:T(8,128)}) %reduce-scatter.2.cloned.1.call-update) | async-done | bytes 131088 | tf_op jit(solution)/shard_map/reduce_scatter | solution.py:72
  (94 shorter events, 92.5 us)
Async XLA Ops:
  9.1 31.3 %all-to-all-start = ((s32[128,1,2]{2,1,0:T(1,128)}), s32[128,1,2]{2,1,0:T(1,128)S(1)}, u32[]{:S(2)}, u32[]{:S(2)}) async-start(s32[128,1,2]{2,1,0:T(1,128)} %bitcast.8), calls=%async_computation | async-start | bytes 131072 | tf_op jit(solution)/shard_map/all_to_all | solution.py:58
  40.4 10.5 copy-start.1
  40.4 234.0 %all-to-all-start.1 = ((f32[128,2,128,128]{3,2,1,0:T(8,128)}), f32[128,2,128,128]{3,2,1,0:T(8,128)}, u32[]{:S(2)}, u32[]{:S(2)}) async-start(f32[128,2,128,128]{3,2,1,0:T(8,128)} %bitcast.39), calls=%async_computation.1 | async-start | bytes 33554432 | tf_op jit(solution)/shard_map/all_to_all | solution.py:51
  50.7 1496.4 %reduce-scatter.2.cloned.1.call-start = ((), (), s32[]{:S(2)}) async-start(), calls=%async_computation.3 | async-start | bytes 16908288 | tf_op jit(solution)/shard_map/reduce_scatter | solution.py:72
  334.7 14.0 copy-start
Sparse Core Ops, SparseCore 0:
  884.3 662.7 reduce-scatter.1
where the time goes:
time: 1560 us; the launch traced here: 1550 us
  waiting for transfers between devices  885 us (57%)
  local copies, waits for them, and re-layouts  335 us (21%)
  matrix products  244 us (16%)
  other arithmetic  54.9 us (4%)
  starting transfers between devices  21.9 us (1%)
    reduce_scatter x1, waiting for transfers between devices, on_device(): lax.psum_scatter(tile_terms(kept, dense_own, weights), ('pair', 'grid'),...  663 us
    dot_general x16, matrix products, tile_block(): jnp.einsum('bfnik,bnjk->bfij', scaled, right_rows, precision=lax.Precisio...  244 us
    all_to_all x1, waiting for transfers between devices, on_device(): lax.all_to_all(send_tiles.reshape(devices, CAP, tile_width, tile_width),...  222 us
    gather x16, local copies, waits for them, and re-layouts, tile_block(): right_rows = dense_own[picked[:, 1]]  146 us
    gather x16, local copies, waits for them, and re-layouts, tile_block(): left_rows = dense_own[picked[:, 0]]  144 us
    scatter-add x1, other arithmetic, on_device(): dense_flat.at[got_target.reshape(-1)]  52.8 us
  transfers between devices with their start and end apart: 3, of which 2 were waited for; matrix products, arithmetic and copies ran while one was open for 1% of the time, Pallas kernels for 0%

commit v1 on v0

v1 whole, which is shorter than its diff:
```python
import functools

import jax
import jax.numpy as jnp
from jax import lax
from jax.experimental import pallas as pl
from jax.experimental.pallas import tpu as pltpu
from jax.sharding import Mesh
from jax.sharding import PartitionSpec as P

NAB = 20
T = 128
FREQS = 2
EXTRA = 8
ALL = ("x", "y", "core", "z")
CHIPS = ("x", "y", "z")
NT = (((1,), (1,)), ((), ()))
MIB = 1024 * 1024


def columns_kernel(groups, tiles_ref, keys_ref, weights_ref, out_ref):
    step = pl.program_id(0)
    flat = out_ref.reshape(T * 8, T)

    @pl.when(step < groups)
    def _():
        for k in range(8):
            flat[pl.ds(k, T, stride=8), :] = tiles_ref[k].T

    @pl.when(step == groups)
    def _():
        out_ref[...] = jnp.zeros_like(out_ref)
        flat[pl.ds(0, T, stride=8), :] = jnp.broadcast_to(keys_ref[...], (T, T))
        flat[pl.ds(1, T, stride=8), :] = weights_ref[...].T


def by_column(b_tiles, keys, weights):
    count = b_tiles.shape[0]
    groups = count // 8
    out = pl.pallas_call(
        functools.partial(columns_kernel, groups),
        grid=(groups + 1,),
        in_specs=[
            pl.BlockSpec((8, T, T), lambda g: (jnp.minimum(g, groups - 1), 0, 0)),
            pl.BlockSpec((1, T), lambda g: (0, 0)),
            pl.BlockSpec((T, T), lambda g: (0, 0)),
        ],
        out_specs=pl.BlockSpec((T, None, 8, T), lambda g: (0, g, 0, 0)),
        out_shape=jax.ShapeDtypeStruct((T, groups + 1, 8, T), jnp.float32),
        name="columns",
    )(b_tiles, keys, weights)
    return out


def expand_kernel(count, blocks, got_ref, bt_ref, w_ref, rows, keys, starts, acc):
    pairs = blocks * T
    chunks = rows.shape[0] - 1
    a = pl.program_id(0)

    @pl.when(a == 0)
    def _():
        per = T // count

        def fill(s, carry):
            x = got_ref[pl.ds(per * s, per), 0:count, :].reshape(T, T).T
            hi = x.astype(jnp.bfloat16)
            rows[s, 0:T, :] = hi
            rows[s, T:, :] = (x - hi.astype(jnp.float32)).astype(jnp.bfloat16)
            key = jnp.sum(got_ref[pl.ds(per * s, per), count, :], axis=0, keepdims=True)
            keys[pl.ds(s, 1), :] = key.astype(jnp.int32)
            return carry

        lax.fori_loop(0, chunks, fill, 0)
        rows[chunks] = jnp.zeros_like(rows[chunks])
        keys[pl.ds(chunks, 8), :] = jnp.full((8, T), -1, jnp.int32)
        w_ref[...] = got_ref[:, count + 1, :].T
        held = keys[0:chunks, :]
        for i in range(NAB + 1):
            starts[i] = jnp.sum((held < i * pairs).astype(jnp.int32))

    first = starts[a]
    last = starts[a + 1]
    base = first // T
    steps = jnp.where(last > first, (last - base * T + 2 * T - 1) // (2 * T), 0)
    acc[...] = jnp.zeros_like(acc)
    place = lax.broadcasted_iota(jnp.int32, (2 * T, 2 * T), 0)

    def add(j, carry):
        s = base + 2 * j
        left = jnp.concatenate([rows[s], rows[s + 1]], axis=1)
        key = jnp.concatenate([keys[pl.ds(s, 1), :], keys[pl.ds(s + 1, 1), :]], axis=1) - a * pairs
        for n in range(pairs // (2 * T)):
            hot = jnp.where(place == key - n * 2 * T, 1.0, 0.0).astype(jnp.bfloat16)
            acc[:, n * 2 * T : (n + 1) * 2 * T] += lax.dot_general(
                left, hot, NT, preferred_element_type=jnp.float32
            )
        return carry

    lax.fori_loop(0, steps, add, 0)
    total = acc[0:T, :] + acc[T:, :]
    hi = total.astype(jnp.bfloat16)
    bt_ref[0:T, :] = hi
    bt_ref[T:, :] = (total - hi.astype(jnp.float32)).astype(jnp.bfloat16)


def expand(got, count, blocks):
    sources = got.shape[0]
    chunks = sources * count // T
    pairs = blocks * T
    return pl.pallas_call(
        functools.partial(expand_kernel, count, blocks),
        grid=(NAB,),
        in_specs=[pl.BlockSpec(memory_space=pltpu.VMEM)],
        out_specs=[
            pl.BlockSpec((None, 2 * T, pairs), lambda a: (a, 0, 0)),
            pl.BlockSpec((T, T), lambda a: (0, 0)),
        ],
        out_shape=[
            jax.ShapeDtypeStruct((NAB, 2 * T, pairs), jnp.bfloat16),
            jax.ShapeDtypeStruct((T, T), jnp.float32),
        ],
        scratch_shapes=[
            pltpu.VMEM((chunks + 1, 2 * T, T), jnp.bfloat16),
            pltpu.VMEM((chunks + 8, T), jnp.int32),
            pltpu.SMEM((NAB + 1,), jnp.int32),
            pltpu.VMEM((2 * T, pairs), jnp.float32),
        ],
        compiler_params=pltpu.CompilerParams(vmem_limit_bytes=40 * MIB),
        name="expand",
    )(got)


def tiles_kernel(blocks, picks, bt_ref, w_ref, out_ref, right_hi, right_lo, first, row_of, slot_of, stage, sems):
    count = picks.shape[0] // 2
    for q in range(NAB + 1):
        first[q] = 0

    def tally(t, carry):
        q = picks[2 * t + 1]
        first[q] = first[q] + 1
        return carry

    lax.fori_loop(0, count, tally, 0)
    total = jnp.int32(0)
    for q in range(NAB + 1):
        here = first[q]
        first[q] = total
        total = total + here

    def arrange(t, carry):
        q = picks[2 * t + 1]
        at = first[q]
        first[q] = at + 1
        row_of[at] = picks[2 * t]
        slot_of[at] = t
        return carry

    lax.fori_loop(0, count, arrange, 0)

    def column(q, begin):
        end = first[q]

        @pl.when(end > begin)
        def _():
            for n in range(blocks):
                lanes = slice(n * T, (n + 1) * T)
                whole = bt_ref[q, 0:T, lanes].astype(jnp.float32) + bt_ref[q, T:, lanes].astype(jnp.float32)
                for f in range(FREQS):
                    scaled = whole * w_ref[f * blocks + n : f * blocks + n + 1, :]
                    hi = scaled.astype(jnp.bfloat16)
                    right_hi[f * T : (f + 1) * T, lanes] = hi
                    right_lo[f * T : (f + 1) * T, lanes] = (scaled - hi.astype(jnp.float32)).astype(jnp.bfloat16)

        def tile(at, carry):
            p = row_of[at]
            t = slot_of[at]
            both = lax.dot_general(bt_ref[p], right_hi[...], NT, preferred_element_type=jnp.float32)
            small = lax.dot_general(bt_ref[p, 0:T, :], right_lo[...], NT, preferred_element_type=jnp.float32)
            result = both[0:T] + (both[T:] + small)
            for f in range(FREQS):
                stage[t, f] = result[:, f * T : (f + 1) * T]
            pltpu.make_async_copy(stage.at[t], out_ref.at[t], sems.at[0]).start()
            return carry

        lax.fori_loop(begin, end, tile, 0)
        return end

    lax.fori_loop(0, NAB, column, jnp.int32(0))
    pltpu.make_async_copy(stage, out_ref, sems.at[0]).wait()


def tiles(picks, bt, w, blocks):
    count = picks.shape[0]
    pairs = blocks * T
    return pl.pallas_call(
        functools.partial(tiles_kernel, blocks),
        grid_spec=pltpu.PrefetchScalarGridSpec(
            num_scalar_prefetch=1,
            grid=(),
            in_specs=[pl.BlockSpec(memory_space=pltpu.VMEM)] * 2,
            out_specs=pl.BlockSpec(memory_space=pl.ANY),
            scratch_shapes=[
                pltpu.VMEM((FREQS * T, pairs), jnp.bfloat16),
                pltpu.VMEM((FREQS * T, pairs), jnp.bfloat16),
                pltpu.SMEM((NAB + 1,), jnp.int32),
                pltpu.SMEM((count,), jnp.int32),
                pltpu.SMEM((count,), jnp.int32),
                pltpu.VMEM((count, FREQS, T, T), jnp.float32),
                pltpu.SemaphoreType.DMA((1,)),
            ],
        ),
        out_shape=jax.ShapeDtypeStruct((count, FREQS, T, T), jnp.float32),
        compiler_params=pltpu.CompilerParams(vmem_limit_bytes=44 * MIB),
        cost_estimate=pl.CostEstimate(
            flops=6 * count * FREQS * T * T * pairs, bytes_accessed=20 * MIB, transcendentals=0
        ),
        name="tiles",
    )(picks.reshape(-1), bt, w)


def on_device(b_tiles, tile_aux, tile_pair, freq_weights, kept):
    count = b_tiles.shape[0]
    devices = lax.axis_size(ALL)
    chips = lax.axis_size(CHIPS)
    me = lax.axis_index(ALL)
    core = lax.axis_index("core")
    blocks = freq_weights.shape[1] // T

    key = tile_aux * (blocks * devices) + (tile_pair % blocks) * devices + tile_pair // blocks
    per = T // count
    lane = jnp.arange(T, dtype=jnp.int32)
    keys = jnp.where(lane // count == me % per, jnp.tile(key, per), 0).astype(jnp.float32)[None]
    weights = jnp.pad(freq_weights.reshape(FREQS * blocks, T), ((0, T - FREQS * blocks), (0, 0)))
    sent = by_column(b_tiles, keys, weights).reshape(devices, count + EXTRA, T)
    got = lax.all_to_all(sent, ALL, split_axis=0, concat_axis=0, tiled=True)

    bt, w = expand(got, count, blocks)
    picks = kept.reshape(lax.axis_size("x") * lax.axis_size("y"), 2, lax.axis_size("z"), 2)
    mine = lax.dynamic_index_in_dim(picks, core, 1, keepdims=False).reshape(chips, 2)
    other = lax.dynamic_index_in_dim(picks, 1 - core, 1, keepdims=False).reshape(chips, 2)
    away = tiles(other, bt, w, blocks)
    landed = lax.ppermute(away, "core", [(0, 1), (1, 0)])
    own = tiles(mine, bt, w, blocks)
    both = own + landed
    parts = lax.all_to_all(both, CHIPS, split_axis=0, concat_axis=0, tiled=True)
    return jnp.sum(parts, axis=0, keepdims=True)


def solution(mesh):
    fine = Mesh(mesh.devices.reshape(4, 4, 2, 4), ALL)
    placed = (P(ALL, None, None), P(ALL), P(ALL), P(None, ALL), P())
    return jax.shard_map(
        on_device, mesh=fine, in_specs=placed, out_specs=P(ALL, None, None, None), check_vma=False
    )
```

time: 1560 us -> 349 us (0.22)
  waiting for transfers between devices: 885 us -> 58.2 us
  local copies, waits for them, and re-layouts: 335 us -> 5.51 us
  matrix products: 244 us -> 0 us
  Pallas kernels: 0 us -> 151 us
  blocking collectives: 0 us -> 100 us
  other arithmetic: 54.9 us -> 17.4 us
    reduce_scatter x1 -> x0, waiting for transfers between devices: 663 us -> none  [on_device(): lax.psum_scatter(tile_terms(kept, dense_own, weights), ('pair', 'grid'),...]
    gather x32 -> x0, local copies, waits for them, and re-layouts: 291 us -> none  [the longest x16 146 us: tile_block(): right_rows = dense_own[picked[:, 1]]]
    dot_general x16 -> x0, matrix products: 244 us -> none  [tile_block(): jnp.einsum('bfnik,bnjk->bfij', scaled, right_rows, precision=lax.Precisio...]
    all_to_all x2 -> x1, waiting for transfers between devices: 222 us -> 58.2 us  [on_device(): got = lax.all_to_all(sent, ALL, split_axis=0, concat_axis=0, tiled=True)]
    pallas_call x0 -> x4, Pallas kernels: none -> 151 us  [the longest x2 110 us: tiles(): pl.pallas_call(functools.partial(tiles_kernel, blocks), grid_spec=pltpu.P...]
    all_to_all x0 -> x1, blocking collectives: none -> 100 us  [on_device(): parts = lax.all_to_all(both, CHIPS, split_axis=0, concat_axis=0, tiled=True)]
    scatter-add x1 -> x0, other arithmetic: 52.8 us -> none  [on_device(): dense_flat.at[got_target.reshape(-1)]]
  transfers between devices with their start and end apart: 3 -> 2, of which waited for: 2 -> 1; matrix products, arithmetic and copies ran while one was open for 1% -> 0% of each run, Pallas kernels for 0% -> 17%
where the time goes in v1:
time: 349 us; the launch traced here: 345 us
  Pallas kernels  151 us (43%)
  blocking collectives  100 us (29%)
  waiting for transfers between devices  58.2 us (17%)
  other arithmetic  17.4 us (5%)
  starting transfers between devices  12.2 us (3%)
  local copies, waits for them, and re-layouts  5.51 us (2%)
    pallas_call x2, Pallas kernels, tiles(): pl.pallas_call(functools.partial(tiles_kernel, blocks), grid_spec=pltpu.P...  110 us
    all_to_all x1, blocking collectives, on_device(): parts = lax.all_to_all(both, CHIPS, split_axis=0, concat_axis=0, tiled=True)  100 us
    all_to_all x1, waiting for transfers between devices, on_device(): got = lax.all_to_all(sent, ALL, split_axis=0, concat_axis=0, tiled=True)  58.2 us
    pallas_call x1, Pallas kernels, expand(): pl.pallas_call(functools.partial(expand_kernel, count, blocks), grid=(NAB...  33.1 us
    all_to_all x1, starting transfers between devices, on_device(): got = lax.all_to_all(sent, ALL, split_axis=0, concat_axis=0, tiled=True)  11.9 us
    add x1, other arithmetic, on_device(): both = own + landed  11.8 us
    pallas_call x1, Pallas kernels, by_column(): pl.pallas_call(functools.partial(columns_kernel, groups), grid=(groups +...  7.68 us
  transfers between devices with their start and end apart: 2, of which 1 were waited for; matrix products, arithmetic and copies ran while one was open for 0% of the time, Pallas kernels for 17%

profile of v1, /device:TPU:1, one launch (start us, length us, event | category | flops | bytes accessed | tf_op | source)
XLA Modules:
  0.0 345.0 jit_solution(3672698699121249724)
XLA Ops:
  0.0 0.7 fusion.3
  0.7 0.1 tile.10
  0.8 0.7 reshape.63
  1.5 0.5 fusion.keys_ref
  2.0 0.6 pad.4.weights_ref
  2.7 0.0 copy-start.1
  2.7 7.7 %columns.1 = f32[128,9,8,128]{3,2,1,0:T(8,128)} custom-call(f32[64,128,128]{2,1,0:T(8,128)} %tiles_ref.1, f32[1,128]{1,0:T(1,128)} %fusion.keys_ref, f32[128,128]{1,0:T(8,128)} %pad.4.weights_ref), custom_call_target="tpu_custom_call" | custom-call | tf_op jit(solution)/shard_map/columns/pallas_call | solution.py:40
  10.4 11.9 %all-to-all-start = ((f32[128,72,128]{2,1,0:T(8,128)}), f32[128,72,128]{2,1,0:T(8,128)}, u32[]{:S(2)}, u32[]{:S(2)}) async-start(f32[128,72,128]{2,1,0:T(8,128)} %bitcast.8), calls=%async_computation | async-start | bytes 9437184 | tf_op jit(solution)/shard_map/all_to_all | solution.py:235
  22.3 0.0 copy-done.1
  22.3 0.1 reshape.62
  22.4 0.2 copy.9
  22.6 0.1 reshape_reshape.7.picks
  22.8 58.2 %all-to-all-done.got_ref = f32[128,72,128]{2,1,0:T(8,128)} async-done(((f32[128,72,128]{2,1,0:T(8,128)}), f32[128,72,128]{2,1,0:T(8,128)}, u32[]{:S(2)}, u32[]{:S(2)}) %all-to-all-start) | async-done | bytes 4718624 | tf_op jit(solution)/shard_map/all_to_all | solution.py:235
  81.0 33.1 %expand.1 = (bf16[20,256,1536]{2,1,0:T(8,128)(2,1)}, f32[128,128]{1,0:T(8,128)S(1)}) custom-call(f32[128,72,128]{2,1,0:T(8,128)} %all-to-all-done.got_ref), custom_call_target="tpu_custom_call" | custom-call | tf_op jit(solution)/shard_map/expand/pallas_call | solution.py:110
  114.1 50.3 %tiles.3 = f32[64,2,128,128]{3,2,1,0:T(8,128)} custom-call(s32[128]{0:T(128)S(1)} %reshape_reshape.7.picks, bf16[20,256,1536]{2,1,0:T(8,128)(2,1)} %get-tuple-element.7.bt_ref, f32[128,128]{1,0:T(8,128)S(1)} %get-tuple-element.8.w_ref), custom_call_target="tpu_custom_call" | custom-call | flops 19327352832 | bytes 20971520 | tf_op jit(solution)/shard_map/tiles/pallas_call | solution.py:195
  164.4 0.3 collective-permute-start
  164.7 0.2 copy.8
  164.9 0.1 reshape_reshape.6.picks
  165.0 60.2 %tiles.2 = f32[64,2,128,128]{3,2,1,0:T(8,128)S(1)} custom-call(s32[128]{0:T(128)S(1)} %reshape_reshape.6.picks, bf16[20,256,1536]{2,1,0:T(8,128)(2,1)} %get-tuple-element.7.bt_ref, f32[128,128]{1,0:T(8,128)S(1)} %get-tuple-element.8.w_ref), custom_call_target="tpu_custom_call" | custom-call | flops 19327352832 | bytes 20971520 | tf_op jit(solution)/shard_map/tiles/pallas_call | solution.py:195
  225.2 0.0 copy-start
  225.2 3.2 copy-done
  228.4 0.0 collective-permute-done
  228.4 11.8 %add.56 = f32[64,2,128,128]{3,2,1,0:T(8,128)} add(f32[64,2,128,128]{3,2,1,0:T(8,128)} %copy-done, f32[64,2,128,128]{3,2,1,0:T(8,128)} %collective-permute-done) | non-fusion elementwise | flops 2097152 | bytes 25165824 | tf_op jit(solution)/shard_map/add | solution.py:244
  240.2 100.4 %all_to_all.10 = f32[64,2,128,128]{3,2,1,0:T(8,128)} all-to-all(f32[64,2,128,128]{3,2,1,0:T(8,128)} %add.56), channel_id=1, replica_groups=mesh['x'=4,'y'=4,'core'=2,'z'=4] {'x','y','z'}, dimensions={0} | all-to-all | bytes 16777216 | tf_op jit(solution)/shard_map/all_to_all | solution.py:245
  340.6 4.4 %reduce_sum.9 = f32[2,128,128]{2,1,0:T(8,128)} reduce(f32[64,2,128,128]{3,2,1,0:T(8,128)} %all_to_all.10, f32[]{:T(128)} %constant.83.clone.1), dimensions={0}, to_apply=%region_0.1 | reduce | flops 2064384 | bytes 8519684 | tf_op jit(solution)/shard_map/reduce_sum | solution.py:246
  (2 shorter events, 0.0 us)
Async XLA Ops:
  2.7 19.6 %copy-start.1 = (s32[128,2]{0,1:T(2,128)S(1)}, s32[128,2]{0,1:T(2,128)}, u32[]{:S(2)}) copy-start(s32[128,2]{0,1:T(2,128)} %param.9) | copy-start | bytes 3076
  10.4 70.6 %all-to-all-start = ((f32[128,72,128]{2,1,0:T(8,128)}), f32[128,72,128]{2,1,0:T(8,128)}, u32[]{:S(2)}, u32[]{:S(2)}) async-start(f32[128,72,128]{2,1,0:T(8,128)} %bitcast.8), calls=%async_computation | async-start | bytes 9437184 | tf_op jit(solution)/shard_map/all_to_all | solution.py:235
  164.4 64.0 %collective-permute-start = (f32[64,2,128,128]{3,2,1,0:T(8,128)}, f32[64,2,128,128]{3,2,1,0:T(8,128)}, u32[]{:S(2)}, u32[]{:S(2)}) collective-permute-start(f32[64,2,128,128]{3,2,1,0:T(8,128)} %tiles.3), channel_id=1, source_target_pairs={{0,4},{4,0},{1,5},{5,1},{2,6},{6,2},{3,7},{7,3},{8,12},{12,8},{9,1... | collective-permute-start | bytes 25165832 | tf_op jit(solution)/shard_map/ppermute | solution.py:242
  225.2 3.2 copy-start

commit v2 on v0

v2 whole, which is shorter than its diff:
```python
import functools

import jax
import jax.numpy as jnp
from jax import lax
from jax.experimental import pallas as pl
from jax.experimental.pallas import tpu as pltpu
from jax.sharding import Mesh
from jax.sharding import PartitionSpec as P

NAB = 20
T = 128
FREQS = 2
EXTRA = 8
FIRST = 4
MIB = 1024 * 1024
GROUP = 4
AHEAD = 8
BF16 = jnp.bfloat16
F32 = jnp.float32


def columns_kernel(groups, blocks, devices, tiles_ref, aux_ref, pair_ref, weights_ref, out_ref):
    step = pl.program_id(0)
    flat = out_ref.reshape(T * 8, T)

    @pl.when(step < groups)
    def _():
        for k in range(8):
            flat[pl.ds(k, T, stride=8), :] = tiles_ref[k].T

    @pl.when(step == groups)
    def _():
        out_ref[...] = jnp.zeros_like(out_ref)
        pair = pair_ref[...].astype(F32)
        source = jnp.floor((pair + 0.5) * (1.0 / blocks))
        key = aux_ref[...].astype(F32) * (blocks * devices) + (pair - source * blocks) * devices + source
        key = jnp.concatenate([key] * (T // key.shape[1]), axis=1)
        flat[pl.ds(0, T, stride=8), :] = jnp.broadcast_to(key, (T, T))
        rows = [weights_ref[f : f + 1, n * T : (n + 1) * T] for f in range(FREQS) for n in range(blocks)]
        rows.append(jnp.zeros((T - FREQS * blocks, T), F32))
        flat[pl.ds(1, T, stride=8), :] = jnp.concatenate(rows, axis=0).T


def by_column(b_tiles, aux, pair, weights, devices):
    count = b_tiles.shape[0]
    groups = count // 8
    blocks = weights.shape[1] // T
    return pl.pallas_call(
        functools.partial(columns_kernel, groups, blocks, devices),
        grid=(groups + 1,),
        in_specs=[
            pl.BlockSpec((8, T, T), lambda g: (jnp.minimum(g, groups - 1), 0, 0)),
            pl.BlockSpec((1, count), lambda g: (0, 0)),
            pl.BlockSpec((1, count), lambda g: (0, 0)),
            pl.BlockSpec(weights.shape, lambda g: (0, 0)),
        ],
        out_specs=pl.BlockSpec((T, None, 8, T), lambda g: (0, g, 0, 0)),
        out_shape=jax.ShapeDtypeStruct((T, groups + 1, 8, T), F32),
        name="columns",
    )(b_tiles, aux[None], pair[None], weights)


def sort_picks(picks, count, first, row_of, column_of, slot_of):
    for q in range(NAB):
        first[q] = 0

    def tally(t, carry):
        q = picks[2 * t + 1]
        first[q] = first[q] + 1
        return carry

    lax.fori_loop(0, count, tally, 0)
    total = jnp.int32(0)
    for q in range(NAB):
        here = first[q]
        first[q] = total
        total = total + here

    def arrange(t, carry):
        q = picks[2 * t + 1]
        at = first[q]
        first[q] = at + 1
        row_of[at] = picks[2 * t]
        column_of[at] = q
        slot_of[at] = t
        return carry

    lax.fori_loop(0, count, arrange, 0)


def multiply(lists, left, right, stage, outs, out_sems, ready):
    row_of, column_of, slot_of = lists
    count = row_of.shape[0]
    share = count // len(outs)

    def group(g, reached):
        reached = ready(reached, column_of[g * GROUP + GROUP - 1] + 1)
        buffer = lax.rem(g, 2)
        done = pltpu.make_async_copy(stage.at[buffer], outs[0].at[pl.ds(0, GROUP)], out_sems.at[buffer])

        @pl.when(g >= 2)
        def _():
            done.wait()

        for k in range(GROUP):
            at = g * GROUP + k
            p = row_of[at]
            q = column_of[at] - 1
            both = jnp.dot(left[p], right[q, 0], preferred_element_type=F32)
            small = jnp.dot(left[p, 0:T, :], right[q, 1], preferred_element_type=F32)
            result = both[0:T] + (both[T:] + small)
            for f in range(FREQS):
                stage[buffer, k, f] = result[:, f * T : (f + 1) * T]
        for k in range(GROUP):
            t = slot_of[g * GROUP + k]
            for i, out in enumerate(outs):

                @pl.when(t // share == i)
                def _():
                    pltpu.make_async_copy(
                        stage.at[buffer, k], out.at[t - i * share], out_sems.at[buffer]
                    ).start()

        return reached

    reached = lax.fori_loop(0, count // GROUP, group, jnp.int32(1))
    ready(reached, NAB)
    for buffer in range(2):
        pltpu.make_async_copy(stage.at[buffer], outs[0].at[pl.ds(0, GROUP)], out_sems.at[buffer]).wait()


def expand_kernel(
    count, blocks, picks, got_ref, left_out, right_out, away_ref, own_ref,
    got, rows, keys, starts, weight, total, left, right, first, row_of, column_of, slot_of, stage,
    got_sems, copy_sems, out_sems,
):
    pairs = blocks * T
    sources = got_ref.shape[0]
    chunks = sources * count // T
    per = T // count
    batch = got.shape[1]
    rounds = sources // batch

    def arrival(r, buffer):
        return pltpu.make_async_copy(
            got_ref.at[pl.ds(r * batch, batch)], got.at[buffer], got_sems.at[buffer]
        )

    for r in range(2):
        arrival(r, r).start()
    sort_picks(picks, picks.shape[0] // 2, first, row_of, column_of, slot_of)
    rows[chunks * T :, :] = jnp.zeros((FIRST * T, 2 * T), BF16)
    keys[pl.ds(chunks, 8), :] = jnp.full((8, T), -1, jnp.int32)

    lanes = lax.broadcasted_iota(jnp.int32, (1, T), 1)

    def fill(r, carry):
        buffer = lax.rem(r, 2)
        arrival(r, buffer).wait()
        here = got.at[buffer]
        for j in range(batch // per):
            s = r * (batch // per) + j
            x = here[j * per : (j + 1) * per, 0:count, :].reshape(T, T)
            hi = x.astype(BF16)
            at = pl.ds(pl.multiple_of(s * T, T), T)
            rows[at, 0:T] = hi
            rows[at, T:] = (x - hi.astype(F32)).astype(BF16)
            key = here[j * per, count : count + 1, :]
            for i in range(1, per):
                key = jnp.where(lanes >= i * count, here[j * per + i, count : count + 1, :], key)
            keys[pl.ds(s, 1), :] = key.astype(jnp.int32)
        spread = here[:, count + 1, :]
        for f in range(FREQS):
            for n in range(blocks):
                lane = f * blocks + n
                weight[f, pl.ds(pl.multiple_of(n * T + r * batch, batch), batch), :] = jnp.broadcast_to(
                    spread[:, lane : lane + 1], (batch, T)
                )

        @pl.when(r + 2 < rounds)
        def _():
            arrival(r + 2, buffer).start()

        return carry

    lax.fori_loop(0, rounds, fill, 0)
    held = keys[0:chunks, :]
    for i in range(NAB + 1):
        starts[i] = jnp.sum((held < i * pairs).astype(jnp.int32))

    half = 2 * T
    wide = FIRST * T
    place = lax.broadcasted_iota(jnp.int32, (half, wide), 0)

    def put(a, n, value):
        at = slice(n * half, (n + 1) * half)

        turned = value.T
        hi = turned.astype(BF16)
        lo = (turned - hi.astype(F32)).astype(BF16)
        row = jnp.minimum(a, NAB - 2)
        left[row, 0:T, at] = hi
        left[row, T:, at] = lo
        slot = jnp.maximum(a, 1) - 1
        for f in range(FREQS):
            scaled = value * weight[f, at, :]
            hi = scaled.astype(BF16)
            cols = slice(f * T, (f + 1) * T)
            right[slot, 0, at, cols] = hi
            right[slot, 1, at, cols] = (scaled - hi.astype(F32)).astype(BF16)

    def column(a, carry):
        begin = starts[a]
        end = starts[a + 1]
        base = (begin // 16) * 16
        chunk = base // T
        more = end - base - wide

        near = jnp.concatenate([keys[pl.ds(chunk + j, 1), :] for j in range(FIRST + 1)], axis=1)
        near = jnp.broadcast_to(near, (8, wide + T))
        near = pltpu.roll(near, wide + T - (base - chunk * T), 1)
        key = near[0:1, 0:wide] - a * pairs
        source = rows[pl.ds(pl.multiple_of(base, 16), wide), :]
        for n in range(pairs // half):
            hot = jnp.where(place == key - n * half, 1.0, 0.0).astype(BF16)
            both = jnp.dot(hot, source, preferred_element_type=F32)
            put(a, n, both[:, 0:T] + both[:, T:])

        @pl.when(more > 0)
        def _():
            total[...] = jnp.zeros_like(total)

            def add(s, carry):
                key = keys[pl.ds(s, 1), :] - a * pairs
                for n in range(pairs // half):
                    hot = jnp.where(place[:, 0:T] == key - n * half, 1.0, 0.0).astype(BF16)
                    both = jnp.dot(
                        hot, rows[pl.ds(pl.multiple_of(s * T, T), T), :], preferred_element_type=F32
                    )
                    total[n * half : (n + 1) * half, :] += both[:, 0:T] + both[:, T:]
                return carry

            lax.fori_loop(chunk, (end + T - 1) // T, add, 0)
            for n in range(pairs // half):
                put(a, n, total[n * half : (n + 1) * half, :])

        @pl.when(a < NAB - 1)
        def _():
            pltpu.make_async_copy(left.at[a], left_out.at[a], copy_sems.at[0]).start()

        @pl.when(a >= 1)
        def _():
            pltpu.make_async_copy(right.at[a - 1], right_out.at[a - 1], copy_sems.at[1]).start()

        return carry

    lax.fori_loop(0, NAB - 2, column, 0)
    column(jnp.int32(NAB - 1), 0)
    column(jnp.int32(NAB - 2), 0)
    multiply(
        (row_of, column_of, slot_of), left, right, stage, (away_ref, own_ref), out_sems, lambda reached, need: need
    )
    pltpu.make_async_copy(left, left_out, copy_sems.at[0]).wait()
    pltpu.make_async_copy(right, right_out, copy_sems.at[1]).wait()


def expand(picks, got, count, blocks):
    sources = got.shape[0]
    chunks = sources * count // T
    pairs = blocks * T
    tiles = picks.shape[0]
    part = jax.ShapeDtypeStruct((tiles // 2, FREQS, T, T), F32)
    return pl.pallas_call(
        functools.partial(expand_kernel, count, blocks),
        grid_spec=pltpu.PrefetchScalarGridSpec(
            num_scalar_prefetch=1,
            grid=(),
            in_specs=[pl.BlockSpec(memory_space=pl.ANY)],
            out_specs=[pl.BlockSpec(memory_space=pl.ANY)] * 4,
            scratch_shapes=[
                pltpu.VMEM((2, 16) + got.shape[1:], F32),
                pltpu.VMEM(((chunks + FIRST) * T, 2 * T), BF16),
                pltpu.VMEM((chunks + 8, T), jnp.int32),
                pltpu.SMEM((NAB + 1,), jnp.int32),
                pltpu.VMEM((FREQS, pairs, T), F32),
                pltpu.VMEM((pairs, T), F32),
                pltpu.VMEM((NAB - 1, 2 * T, pairs), BF16),
                pltpu.VMEM((NAB - 1, 2, pairs, FREQS * T), BF16),
                pltpu.SMEM((NAB,), jnp.int32),
                pltpu.SMEM((tiles,), jnp.int32),
                pltpu.SMEM((tiles,), jnp.int32),
                pltpu.SMEM((tiles,), jnp.int32),
                pltpu.VMEM((2, GROUP, FREQS, T, T), F32),
                pltpu.SemaphoreType.DMA((2,)),
                pltpu.SemaphoreType.DMA((2,)),
                pltpu.SemaphoreType.DMA((2,)),
            ],
        ),
        out_shape=[
            jax.ShapeDtypeStruct((NAB - 1, 2 * T, pairs), BF16),
            jax.ShapeDtypeStruct((NAB - 1, 2, pairs, FREQS * T), BF16),
            part,
            part,
        ],
        compiler_params=pltpu.CompilerParams(vmem_limit_bytes=58 * MIB),
        name="expand",
    )(picks.reshape(-1), got)


def tiles_kernel(
    picks, left_ref, right_ref, away_ref, own_ref,
    left, right, first, row_of, column_of, slot_of, stage, left_sems, right_sems, out_sems,
):
    def fetch(q):
        return (
            pltpu.make_async_copy(left_ref.at[q - 1], left.at[q - 1], left_sems.at[q - 1]),
            pltpu.make_async_copy(right_ref.at[q - 1], right.at[q - 1], right_sems.at[q - 1]),
        )

    for q in range(1, AHEAD + 1):
        for copy in fetch(q):
            copy.start()
    sort_picks(picks, picks.shape[0] // 2, first, row_of, column_of, slot_of)

    def await_column(q, carry):
        @pl.when(q + AHEAD < NAB)
        def _():
            for copy in fetch(q + AHEAD):
                copy.start()

        for copy in fetch(q):
            copy.wait()
        return carry

    def ready(reached, need):
        lax.fori_loop(reached, need, await_column, 0)
        return need

    multiply((row_of, column_of, slot_of), left, right, stage, (away_ref, own_ref), out_sems, ready)


def tiles(picks, left, right):
    count = picks.shape[0]
    pairs = left.shape[2]
    part = jax.ShapeDtypeStruct((count // 2, FREQS, T, T), F32)
    return pl.pallas_call(
        tiles_kernel,
        grid_spec=pltpu.PrefetchScalarGridSpec(
            num_scalar_prefetch=1,
            grid=(),
            in_specs=[pl.BlockSpec(memory_space=pl.ANY)] * 2,
            out_specs=[pl.BlockSpec(memory_space=pl.ANY)] * 2,
            scratch_shapes=[
                pltpu.VMEM((NAB - 1, 2 * T, pairs), BF16),
                pltpu.VMEM((NAB - 1, 2, pairs, FREQS * T), BF16),
                pltpu.SMEM((NAB,), jnp.int32),
                pltpu.SMEM((count,), jnp.int32),
                pltpu.SMEM((count,), jnp.int32),
                pltpu.SMEM((count,), jnp.int32),
                pltpu.VMEM((2, GROUP, FREQS, T, T), F32),
                pltpu.SemaphoreType.DMA((NAB - 1,)),
                pltpu.SemaphoreType.DMA((NAB - 1,)),
                pltpu.SemaphoreType.DMA((2,)),
            ],
        ),
        out_shape=[part, part],
        compiler_params=pltpu.CompilerParams(vmem_limit_bytes=56 * MIB),
        cost_estimate=pl.CostEstimate(
            flops=6 * count * FREQS * T * T * pairs, bytes_accessed=56 * MIB, transcendentals=0
        ),
        name="tiles",
    )(picks.reshape(-1), left, right)


def layout(me, owner):
    plane = jnp.arange(16, dtype=jnp.int32)
    high, low = plane // 4, plane % 4
    here = jnp.where(owner == 0, me % 4, me // 32)
    lists = []
    for step in (2, 1, 3, 0):
        at = (here + step) % 4
        lists.append(
            jnp.where(owner == 0, ((high * 4 + low) * 2) * 4 + at, ((at * 4 + high) * 2 + 1) * 4 + low)
        )
    return lists


def shift(step):
    pairs = []
    for d in range(128):
        x, y, core, z = d // 32, d // 8 % 4, d // 4 % 2, d % 4
        if core == 0:
            z = (z + step) % 4
        else:
            x = (x + step) % 4
        pairs.append((d, ((x * 4 + y) * 2 + core) * 4 + z))
    return pairs


PLANES = [[(plane * 2) * 4 + z for plane in range(16)] for z in range(4)] + [
    [((x * 4 + plane // 4) * 2 + 1) * 4 + plane % 4 for plane in range(16)] for x in range(4)
]
SWAP = [(d, d ^ 4) for d in range(128)]


def on_device(b_tiles, tile_aux, tile_pair, freq_weights, kept):
    count = b_tiles.shape[0]
    devices = lax.axis_size("d")
    me = lax.axis_index("d")
    core = me // 4 % 2
    blocks = freq_weights.shape[1] // T

    sent = by_column(b_tiles, tile_aux, tile_pair, freq_weights, devices).reshape(devices, count + EXTRA, T)
    got = lax.all_to_all(sent, "d", split_axis=0, concat_axis=0, tiled=True)

    lists = [layout(me, owner) for owner in (1 - core, core)]
    picks = kept[
        jnp.concatenate(
            [part for far, up, down, keep in lists for part in (far, up[:8], down[:8])]
            + [part for far, up, down, keep in lists for part in (up[8:], down[8:], keep)]
        )
    ]
    left, right, away, own = expand(picks[:64], got, count, blocks)
    landed = lax.ppermute(away, "d", SWAP)
    leaving = [own[n] + landed[n] for n in (slice(0, 16), slice(16, 24), slice(24, 32))]
    left, right, leaving = lax.optimization_barrier((left, right, leaving))
    far = lax.ppermute(leaving[0], "d", shift(2))
    up_a = lax.ppermute(leaving[1], "d", shift(1))
    down_a = lax.ppermute(leaving[2], "d", shift(-1))

    away, own = tiles(picks[64:], left, right)
    away, far, up_a, down_a = lax.optimization_barrier((away, far, up_a, down_a))
    landed = lax.ppermute(away, "d", SWAP)
    up_b = lax.ppermute(own[0:8] + landed[0:8], "d", shift(1))
    down_b = lax.ppermute(own[8:16] + landed[8:16], "d", shift(-1))
    summed = jnp.concatenate(
        [
            own[16:24] + landed[16:24] + far[0:8] + up_a + down_a,
            own[24:32] + landed[24:32] + far[8:16] + up_b + down_b,
        ]
    )
    parts = lax.all_to_all(summed, "d", split_axis=0, concat_axis=0, tiled=True, axis_index_groups=PLANES)
    return jnp.sum(parts, axis=0, keepdims=True)


def solution(mesh):
    flat = Mesh(mesh.devices.reshape(-1), ("d",))
    placed = (P("d", None, None), P("d"), P("d"), P(None, "d"), P())
    return jax.shard_map(
        on_device, mesh=flat, in_specs=placed, out_specs=P("d", None, None, None), check_vma=False
    )
```

time: 1560 us -> 237 us (0.15)
  waiting for transfers between devices: 885 us -> 89 us
  local copies, waits for them, and re-layouts: 335 us -> 2.46 us
  matrix products: 244 us -> 0 us
  Pallas kernels: 0 us -> 85.2 us
  other arithmetic: 54.9 us -> 8.29 us
  blocking collectives: 0 us -> 31.2 us
    reduce_scatter x1 -> x0, waiting for transfers between devices: 663 us -> none  [on_device(): lax.psum_scatter(tile_terms(kept, dense_own, weights), ('pair', 'grid'),...]
    gather x32 -> x1, local copies, waits for them, and re-layouts: 291 us -> 0.64 us  [on_device(): kept[jnp.concatenate([part for far, up, down, keep in lists for part in (...]
    dot_general x16 -> x0, matrix products: 244 us -> none  [tile_block(): jnp.einsum('bfnik,bnjk->bfij', scaled, right_rows, precision=lax.Precisio...]
    all_to_all x2 -> x1, waiting for transfers between devices: 222 us -> 56.6 us  [on_device(): got = lax.all_to_all(sent, 'd', split_axis=0, concat_axis=0, tiled=True)]
    pallas_call x0 -> x3, Pallas kernels: none -> 85.2 us  [the longest x1 49.5 us: expand(): pl.pallas_call(functools.partial(expand_kernel, count, blocks), grid_spec...]
    scatter-add x1 -> x0, other arithmetic: 52.8 us -> none  [on_device(): dense_flat.at[got_target.reshape(-1)]]
    ppermute x0 -> x7, waiting for transfers between devices: none -> 32.3 us  [the longest x2 14 us: on_device(): landed = lax.ppermute(away, 'd', SWAP)]
    all_to_all x0 -> x1, blocking collectives: none -> 31.2 us  [on_device(): lax.all_to_all(summed, 'd', split_axis=0, concat_axis=0, tiled=True, axis...]
  transfers between devices with their start and end apart: 3 -> 8, of which waited for: 2 -> 5; matrix products, arithmetic and copies ran while one was open for 1% -> 1% of each run, Pallas kernels for 0% -> 12%
where the time goes in v2:
time: 237 us; the launch traced here: 236 us
  waiting for transfers between devices  89 us (38%)
  Pallas kernels  85.2 us (36%)
  blocking collectives  31.2 us (13%)
  starting transfers between devices  19.8 us (8%)
  other arithmetic  8.29 us (3%)
  local copies, waits for them, and re-layouts  2.46 us (1%)
    all_to_all x1, waiting for transfers between devices, on_device(): got = lax.all_to_all(sent, 'd', split_axis=0, concat_axis=0, tiled=True)  56.6 us
    pallas_call x1, Pallas kernels, expand(): pl.pallas_call(functools.partial(expand_kernel, count, blocks), grid_spec...  49.5 us
    all_to_all x1, blocking collectives, on_device(): lax.all_to_all(summed, 'd', split_axis=0, concat_axis=0, tiled=True, axis...  31.2 us
    pallas_call x1, Pallas kernels, tiles(): pl.pallas_call(tiles_kernel, grid_spec=pltpu.PrefetchScalarGridSpec(num_s...  28.1 us
    ppermute x2, waiting for transfers between devices, on_device(): landed = lax.ppermute(away, 'd', SWAP)  14 us
    ppermute x1, waiting for transfers between devices, on_device(): up_b = lax.ppermute(own[0:8] + landed[0:8], 'd', shift(1))  12.5 us
    all_to_all x1, starting transfers between devices, on_device(): got = lax.all_to_all(sent, 'd', split_axis=0, concat_axis=0, tiled=True)  11.9 us
    pallas_call x1, Pallas kernels, by_column(): pl.pallas_call(functools.partial(columns_kernel, groups, blocks, devices)...  7.62 us
  transfers between devices with their start and end apart: 8, of which 5 were waited for; matrix products, arithmetic and copies ran while one was open for 1% of the time, Pallas kernels for 12%

profile of v2, /device:TPU:1, one launch (start us, length us, event | category | flops | bytes accessed | tf_op | source)
XLA Modules:
  0.0 236.3 jit_solution(13737578898275492482)
XLA Ops:
  0.0 7.6 %columns.1 = f32[128,9,8,128]{3,2,1,0:T(8,128)} custom-call(f32[64,128,128]{2,1,0:T(8,128)} %tiles_ref.1, s32[1,64]{1,0:T(1,128)} %bitcast.31, s32[1,64]{1,0:T(1,128)} %bitcast.32, f32[2,1536]{1,0:T(2,128)} %weights_ref.1), custom_call_target="tpu_custom_call" | custom-call | tf_op jit(solution)/shard_map/columns/pallas_call | solution.py:49
  7.6 0.0 copy-start.2
  7.6 11.9 %all-to-all-start = ((f32[128,72,128]{2,1,0:T(8,128)}), f32[128,72,128]{2,1,0:T(8,128)}, u32[]{:S(2)}, u32[]{:S(2)}) async-start(f32[128,72,128]{2,1,0:T(8,128)} %bitcast.30), calls=%async_computation | async-start | bytes 9437184 | tf_op jit(solution)/shard_map/all_to_all | solution.py:415
  19.7 0.0 copy-done.2
  19.7 0.1 copy.7
  19.9 0.1 slice_bitcast_fusion.2
  20.0 0.1 slice_bitcast_fusion
  20.0 0.1 slice_bitcast_fusion.3
  20.1 0.1 slice_bitcast_fusion.1
  20.2 0.1 concatenate.61
  20.3 0.6 gather_fusion
  21.0 0.7 reshape.403.picks
  21.6 56.6 %all-to-all-done.got_ref = f32[128,72,128]{2,1,0:T(8,128)} async-done(((f32[128,72,128]{2,1,0:T(8,128)}), f32[128,72,128]{2,1,0:T(8,128)}, u32[]{:S(2)}, u32[]{:S(2)}) %all-to-all-start) | async-done | bytes 4718624 | tf_op jit(solution)/shard_map/all_to_all | solution.py:415
  78.3 49.5 %expand.1 = (bf16[19,256,1536]{2,1,0:T(8,128)(2,1)}, bf16[19,2,1536,256]{3,2,1,0:T(8,128)(2,1)}, f32[32,2,128,128]{3,2,1,0:T(8,128)}, f32[32,2,128,128]{3,2,1,0:T(8,128)}) custom-call(s32[128]{0:T(128)} %reshape.403.picks, f32[128,72,128]{2,1,0:T(8,128)} %all-to-all-done.got_ref), custom_call_target="tpu_custom_call" | custom-call | tf_op jit(solution)/shard_map/expand/pallas_call | solution.py:274
  127.8 0.0 copy-start
  127.8 0.6 collective-permute-start
  128.4 7.0 %collective-permute-done = f32[32,2,128,128]{3,2,1,0:T(8,128)S(1)} collective-permute-done((f32[32,2,128,128]{3,2,1,0:T(8,128)}, f32[32,2,128,128]{3,2,1,0:T(8,128)S(1)}, u32[]{:S(2)}, u32[]{:S(2)}) %collective-permute-start) | collective-permute-done | bytes 4194336 | tf_op jit(solution)/shard_map/ppermute | solution.py:425
  135.4 1.8 slice_add_fusion
  137.2 0.0 copy-done
  137.2 1.2 slice_add_fusion.5
  138.4 0.6 collective-permute-start.1
  139.0 0.6 reshape.402.picks
  139.7 1.9 collective-permute-start.2
  141.5 0.8 collective-permute-start.3
  142.3 28.1 %tiles.1 = (f32[32,2,128,128]{3,2,1,0:T(8,128)}, f32[32,2,128,128]{3,2,1,0:T(8,128)}) custom-call(s32[128]{0:T(128)} %reshape.402.picks, bf16[19,256,1536]{2,1,0:T(8,128)(2,1)} %get-tuple-element.24.left_ref, bf16[19,2,1536,256]{3,2,1,0:T(8,128)(2,1)} %get-tuple-element.25.right_ref), custom_call_target="tpu_custom_call" | custom-call | flops 19327352832 | bytes 58720256 | tf_op jit(solution)/shard_map/tiles/pallas_call | solution.py:347
  170.5 0.0 copy-start.1
  170.5 5.8 %collective-permute-done.2 = f32[8,2,128,128]{3,2,1,0:T(8,128)S(1)} collective-permute-done((f32[8,2,128,128]{3,2,1,0:T(8,128)}, f32[8,2,128,128]{3,2,1,0:T(8,128)S(1)}, u32[]{:S(2)}, u32[]{:S(2)}) %collective-permute-start.2) | collective-permute-done | bytes 1048608 | tf_op jit(solution)/shard_map/ppermute | solution.py:429
  176.3 0.0 collective-permute-done.3
  176.3 0.0 collective-permute-done.1
  176.3 1.2 collective-permute-start.4
  177.6 7.0 %collective-permute-done.4 = f32[32,2,128,128]{3,2,1,0:T(8,128)S(1)} collective-permute-done((f32[32,2,128,128]{3,2,1,0:T(8,128)}, f32[32,2,128,128]{3,2,1,0:T(8,128)S(1)}, u32[]{:S(2)}, u32[]{:S(2)}) %collective-permute-start.4) | collective-permute-done | bytes 4194336 | tf_op jit(solution)/shard_map/ppermute | solution.py:434
  184.6 1.8 slice_add_fusion.2
  186.3 0.2 collective-permute-start.5
  186.5 2.5 %collective-permute-start.6 = (f32[8,2,128,128]{3,2,1,0:T(8,128)S(1)}, f32[8,2,128,128]{3,2,1,0:T(8,128)S(1)}, u32[]{:S(2)}, u32[]{:S(2)}) collective-permute-start(f32[8,2,128,128]{3,2,1,0:T(8,128)S(1)} %get-tuple-element.38), channel_id=1, source_target_pairs={{0,3},{1,0},{2,1},{3,2},{4,100},{5,101},{6,102},{7,103},{8,11},{9,... | collective-permute-start | bytes 3145736 | tf_op jit(solution)/shard_map/ppermute | solution.py:436
  189.1 12.5 %collective-permute-done.5 = f32[8,2,128,128]{3,2,1,0:T(8,128)S(1)} collective-permute-done((f32[8,2,128,128]{3,2,1,0:T(8,128)S(1)}, f32[8,2,128,128]{3,2,1,0:T(8,128)S(1)}, u32[]{:S(2)}, u32[]{:S(2)}) %collective-permute-start.5) | collective-permute-done | bytes 1048608 | tf_op jit(solution)/shard_map/ppermute | solution.py:435
  201.5 0.0 collective-permute-done.6
  201.5 0.0 copy-done.1
  201.6 2.5 %fusion.5 = (f32[8,2,128,128]{3,2,1,0:T(8,128)S(1)}, f32[8,2,128,128]{3,2,1,0:T(8,128)S(1)}) fusion(f32[8,2,128,128]{3,2,1,0:T(8,128)S(1)} %collective-permute-done.3, f32[8,2,128,128]{3,2,1,0:T(8,128)S(1)} %collective-permute-done.2, f32[32,2,128,128]{3,2,1,0:T(8,128)S(1)} %collective-permute-done.4, f32[16,2,128,128]{3,2,1,0:T(8,128)} %collective-permute-done.1, ...), kind=kLoop, calls=%fused_computation.12 | loop fusion | flops 2097152 | bytes 12582912 | tf_op jit(solution)/shard_map/add | solution.py:439
  204.0 0.2 pad_maximum_fusion
  204.2 31.2 %all_to_all.10 = f32[16,2,128,128]{3,2,1,0:T(8,128)S(1)} all-to-all(f32[16,2,128,128]{3,2,1,0:T(8,128)S(1)} %pad_maximum_fusion), channel_id=1, replica_groups={{0,8,16,24,32,40,48,56,64,72,80,88,96,104,112,120},{1,9,17,25,33,41,49,..., dimensions={0} | all-to-all | bytes 4194304 | tf_op jit(solution)/shard_map/all_to_all | solution.py:443
  235.5 0.8 reduce_sum.9
  (7 shorter events, 0.1 us)
Async XLA Ops:
  7.6 12.1 %copy-start.2 = (s32[128,2]{0,1:T(2,128)S(1)}, s32[128,2]{0,1:T(2,128)}, u32[]{:S(2)}) copy-start(s32[128,2]{0,1:T(2,128)} %param.9) | copy-start | bytes 3076
  7.6 70.6 %all-to-all-start = ((f32[128,72,128]{2,1,0:T(8,128)}), f32[128,72,128]{2,1,0:T(8,128)}, u32[]{:S(2)}, u32[]{:S(2)}) async-start(f32[128,72,128]{2,1,0:T(8,128)} %bitcast.30), calls=%async_computation | async-start | bytes 9437184 | tf_op jit(solution)/shard_map/all_to_all | solution.py:415
  127.8 9.4 %copy-start = (f32[32,2,128,128]{3,2,1,0:T(8,128)S(1)}, f32[32,2,128,128]{3,2,1,0:T(8,128)}, u32[]{:S(2)}) copy-start(f32[32,2,128,128]{3,2,1,0:T(8,128)} %get-tuple-element.22) | copy-start | bytes 12582916
  127.8 7.6 %collective-permute-start = (f32[32,2,128,128]{3,2,1,0:T(8,128)}, f32[32,2,128,128]{3,2,1,0:T(8,128)S(1)}, u32[]{:S(2)}, u32[]{:S(2)}) collective-permute-start(f32[32,2,128,128]{3,2,1,0:T(8,128)} %get-tuple-element.23), channel_id=1, source_target_pairs={{0,4},{1,5},{2,6},{3,7},{4,0},{5,1},{6,2},{7,3},{8,12},{9,13},{10,... | collective-permute-start | bytes 12582920 | tf_op jit(solution)/shard_map/ppermute | solution.py:425
  138.4 37.9 %collective-permute-start.1 = (f32[16,2,128,128]{3,2,1,0:T(8,128)S(1)}, f32[16,2,128,128]{3,2,1,0:T(8,128)}, u32[]{:S(2)}, u32[]{:S(2)}) collective-permute-start(f32[16,2,128,128]{3,2,1,0:T(8,128)S(1)} %slice_add_fusion), channel_id=1, source_target_pairs={{0,2},{1,3},{2,0},{3,1},{4,68},{5,69},{6,70},{7,71},{8,10},{9,11},... | collective-permute-start | bytes 6291464 | tf_op jit(solution)/shard_map/ppermute | solution.py:428
  139.7 36.7 %collective-permute-start.2 = (f32[8,2,128,128]{3,2,1,0:T(8,128)}, f32[8,2,128,128]{3,2,1,0:T(8,128)S(1)}, u32[]{:S(2)}, u32[]{:S(2)}) collective-permute-start(f32[8,2,128,128]{3,2,1,0:T(8,128)} %get-tuple-element.29), channel_id=1, source_target_pairs={{0,1},{1,2},{2,3},{3,0},{4,36},{5,37},{6,38},{7,39},{8,9},{9,10},{... | collective-permute-start | bytes 3145736 | tf_op jit(solution)/shard_map/ppermute | solution.py:429
  141.5 34.8 %collective-permute-start.3 = (f32[8,2,128,128]{3,2,1,0:T(8,128)S(1)}, f32[8,2,128,128]{3,2,1,0:T(8,128)S(1)}, u32[]{:S(2)}, u32[]{:S(2)}) collective-permute-start(f32[8,2,128,128]{3,2,1,0:T(8,128)S(1)} %get-tuple-element.30), channel_id=1, source_target_pairs={{0,3},{1,0},{2,1},{3,2},{4,100},{5,101},{6,102},{7,103},{8,11},{9,... | collective-permute-start | bytes 3145736 | tf_op jit(solution)/shard_map/ppermute | solution.py:430
  170.5 31.1 %copy-start.1 = (f32[32,2,128,128]{3,2,1,0:T(8,128)S(1)}, f32[32,2,128,128]{3,2,1,0:T(8,128)}, u32[]{:S(2)}) copy-start(f32[32,2,128,128]{3,2,1,0:T(8,128)} %get-tuple-element.26) | copy-start | bytes 12582916
  176.3 8.2 %collective-permute-start.4 = (f32[32,2,128,128]{3,2,1,0:T(8,128)}, f32[32,2,128,128]{3,2,1,0:T(8,128)S(1)}, u32[]{:S(2)}, u32[]{:S(2)}) collective-permute-start(f32[32,2,128,128]{3,2,1,0:T(8,128)} %get-tuple-element.31), channel_id=1, source_target_pairs={{0,4},{1,5},{2,6},{3,7},{4,0},{5,1},{6,2},{7,3},{8,12},{9,13},{10,... | collective-permute-start | bytes 12582920 | tf_op jit(solution)/shard_map/ppermute | solution.py:434
  186.3 15.2 %collective-permute-start.5 = (f32[8,2,128,128]{3,2,1,0:T(8,128)S(1)}, f32[8,2,128,128]{3,2,1,0:T(8,128)S(1)}, u32[]{:S(2)}, u32[]{:S(2)}) collective-permute-start(f32[8,2,128,128]{3,2,1,0:T(8,128)S(1)} %get-tuple-element.37), channel_id=1, source_target_pairs={{0,1},{1,2},{2,3},{3,0},{4,36},{5,37},{6,38},{7,39},{8,9},{9,10},{... | collective-permute-start | bytes 3145736 | tf_op jit(solution)/shard_map/ppermute | solution.py:435
  186.5 15.0 %collective-permute-start.6 = (f32[8,2,128,128]{3,2,1,0:T(8,128)S(1)}, f32[8,2,128,128]{3,2,1,0:T(8,128)S(1)}, u32[]{:S(2)}, u32[]{:S(2)}) collective-permute-start(f32[8,2,128,128]{3,2,1,0:T(8,128)S(1)} %get-tuple-element.38), channel_id=1, source_target_pairs={{0,3},{1,0},{2,1},{3,2},{4,100},{5,101},{6,102},{7,103},{8,11},{9,... | collective-permute-start | bytes 3145736 | tf_op jit(solution)/shard_map/ppermute | solution.py:436

commit v3 on v2

v3 whole, which is shorter than its diff:
```python
import functools

import jax
import jax.numpy as jnp
from jax import lax
from jax.experimental import pallas as pl
from jax.experimental.pallas import tpu as pltpu
from jax.sharding import Mesh
from jax.sharding import PartitionSpec as P

NAB = 20
T = 128
FREQS = 2
EXTRA = 8
FIRST = 4
MIB = 1024 * 1024
ARRIVING = 4
BATCH = 16
GROUP = 16
BF16 = jnp.bfloat16
F32 = jnp.float32


def columns_kernel(groups, blocks, devices, tiles_ref, aux_ref, pair_ref, weights_ref, out_ref):
    step = pl.program_id(0)
    flat = out_ref.reshape(T * 8, T)

    @pl.when(step < groups)
    def _():
        for k in range(8):
            flat[pl.ds(k, T, stride=8), :] = tiles_ref[k].T

    @pl.when(step == groups)
    def _():
        out_ref[...] = jnp.zeros_like(out_ref)
        pair = pair_ref[...].astype(F32)
        source = jnp.floor((pair + 0.5) * (1.0 / blocks))
        key = aux_ref[...].astype(F32) * (blocks * devices) + (pair - source * blocks) * devices + source
        key = jnp.concatenate([key] * (T // key.shape[1]), axis=1)
        flat[pl.ds(0, T, stride=8), :] = jnp.broadcast_to(key, (T, T))
        rows = [weights_ref[f : f + 1, n * T : (n + 1) * T] for f in range(FREQS) for n in range(blocks)]
        rows.append(jnp.zeros((T - FREQS * blocks, T), F32))
        flat[pl.ds(1, T, stride=8), :] = jnp.concatenate(rows, axis=0).T


def by_column(b_tiles, aux, pair, weights, devices):
    count = b_tiles.shape[0]
    groups = count // 8
    blocks = weights.shape[1] // T
    return pl.pallas_call(
        functools.partial(columns_kernel, groups, blocks, devices),
        grid=(groups + 1,),
        in_specs=[
            pl.BlockSpec((8, T, T), lambda g: (jnp.minimum(g, groups - 1), 0, 0)),
            pl.BlockSpec((1, count), lambda g: (0, 0)),
            pl.BlockSpec((1, count), lambda g: (0, 0)),
            pl.BlockSpec(weights.shape, lambda g: (0, 0)),
        ],
        out_specs=pl.BlockSpec((T, None, 8, T), lambda g: (0, g, 0, 0)),
        out_shape=jax.ShapeDtypeStruct((T, groups + 1, 8, T), F32),
        name="columns",
    )(b_tiles, aux[None], pair[None], weights)


def multiply(picks, left, right, stage, outs, out_sems):
    share = outs[0].shape[0]

    def copies(g):
        buffer = lax.rem(g, 2)
        at = pl.ds(lax.rem(g, share // GROUP) * GROUP, GROUP)
        return [pltpu.make_async_copy(stage.at[buffer], out.at[at], out_sems.at[buffer]) for out in outs]

    def group(g, carry):
        buffer = lax.rem(g, 2)

        @pl.when(g >= 2)
        def _():
            copies(g)[0].wait()

        for k in range(GROUP):
            p = picks[2 * (g * GROUP + k)]
            q = picks[2 * (g * GROUP + k) + 1]
            both = jnp.dot(left[p], right[q, 0], preferred_element_type=F32)
            small = jnp.dot(left[p, 0:T, :], right[q, 1], preferred_element_type=F32)
            result = both[0:T] + (both[T:] + small)
            for f in range(FREQS):
                stage[buffer, k, f] = result[:, f * T : (f + 1) * T]
        for i, copy in enumerate(copies(g)):

            @pl.when(g // (share // GROUP) == i)
            def _():
                copy.start()

        return carry

    lax.fori_loop(0, len(outs) * share // GROUP, group, 0)
    for g in range(2):
        copies(g)[0].wait()


def products_kernel(count, blocks, shares, picks, got_ref, *refs):
    outs, (
        got, rows, keys, starts, weight, total, left, right, stage,
        got_sems, out_sems,
    ) = refs[:shares], refs[shares:]
    pairs = blocks * T
    sources = got_ref.shape[0]
    chunks = sources * count // T
    per = T // count
    batch = got.shape[1]
    rounds = sources // batch

    def arrival(r, buffer):
        return pltpu.make_async_copy(
            got_ref.at[pl.ds(r * batch, batch)], got.at[buffer], got_sems.at[buffer]
        )

    for r in range(ARRIVING):
        arrival(r, r).start()
    rows[chunks * T :, :] = jnp.zeros((FIRST * T, 2 * T), BF16)
    keys[pl.ds(chunks, 8), :] = jnp.full((8, T), -1, jnp.int32)

    lanes = lax.broadcasted_iota(jnp.int32, (1, T), 1)

    def fill(r, carry):
        buffer = lax.rem(r, ARRIVING)
        arrival(r, buffer).wait()
        here = got.at[buffer]
        for j in range(batch // per):
            s = r * (batch // per) + j
            x = here[j * per : (j + 1) * per, 0:count, :].reshape(T, T)
            hi = x.astype(BF16)
            at = pl.ds(pl.multiple_of(s * T, T), T)
            rows[at, 0:T] = hi
            rows[at, T:] = (x - hi.astype(F32)).astype(BF16)
            key = here[j * per, count : count + 1, :]
            for i in range(1, per):
                key = jnp.where(lanes >= i * count, here[j * per + i, count : count + 1, :], key)
            keys[pl.ds(s, 1), :] = key.astype(jnp.int32)
        spread = here[:, count + 1, :]
        for f in range(FREQS):
            for n in range(blocks):
                lane = f * blocks + n
                weight[f, pl.ds(pl.multiple_of(n * T + r * batch, batch), batch), :] = jnp.broadcast_to(
                    spread[:, lane : lane + 1], (batch, T)
                )

        @pl.when(r + ARRIVING < rounds)
        def _():
            arrival(r + ARRIVING, buffer).start()

        return carry

    lax.fori_loop(0, rounds, fill, 0)
    held = keys[0:chunks, :]
    for i in range(NAB + 1):
        starts[i] = jnp.sum((held < i * pairs).astype(jnp.int32))

    half = 2 * T
    wide = FIRST * T
    place = lax.broadcasted_iota(jnp.int32, (half, wide), 0)

    def put(a, n, value):
        at = slice(n * half, (n + 1) * half)

        turned = value.T
        hi = turned.astype(BF16)
        lo = (turned - hi.astype(F32)).astype(BF16)
        left[a, 0:T, at] = hi
        left[a, T:, at] = lo
        for f in range(FREQS):
            scaled = value * weight[f, at, :]
            hi = scaled.astype(BF16)
            cols = slice(f * T, (f + 1) * T)
            right[a, 0, at, cols] = hi
            right[a, 1, at, cols] = (scaled - hi.astype(F32)).astype(BF16)

    def straight(a):
        begin = starts[a]
        base = (begin // 16) * 16
        chunk = base // T
        near = jnp.concatenate([keys[pl.ds(chunk + j, 1), :] for j in range(FIRST + 1)], axis=1)
        near = jnp.broadcast_to(near, (8, wide + T))
        near = pltpu.roll(near, wide + T - (base - chunk * T), 1)
        key = near[0:1, 0:wide] - a * pairs
        source = rows[pl.ds(pl.multiple_of(base, 16), wide), :]
        for n in range(pairs // half):
            hot = jnp.where(place == key - n * half, 1.0, 0.0).astype(BF16)
            both = jnp.dot(hot, source, preferred_element_type=F32)
            put(a, n, both[:, 0:T] + both[:, T:])

    def whole(a):
        chunk = starts[a] // T
        end = starts[a + 1]

        @pl.when(end - (starts[a] // 16) * 16 > wide)
        def _():
            total[...] = jnp.zeros_like(total)

            def add(s, carry):
                key = keys[pl.ds(s, 1), :] - a * pairs
                for n in range(pairs // half):
                    hot = jnp.where(place[:, 0:T] == key - n * half, 1.0, 0.0).astype(BF16)
                    both = jnp.dot(
                        hot, rows[pl.ds(pl.multiple_of(s * T, T), T), :], preferred_element_type=F32
                    )
                    total[n * half : (n + 1) * half, :] += both[:, 0:T] + both[:, T:]
                return carry

            lax.fori_loop(chunk, (end + T - 1) // T, add, 0)
            for n in range(pairs // half):
                put(a, n, total[n * half : (n + 1) * half, :])

    def columns(i, carry):
        pair = 2 * i, 2 * i + 1
        for a in pair:
            straight(a)
        for a in pair:
            whole(a)
        return carry

    lax.fori_loop(0, NAB // 2, columns, 0)
    multiply(picks, left, right, stage, outs, out_sems)


def products(picks, shares, got, count, blocks):
    sources = got.shape[0]
    chunks = sources * count // T
    pairs = blocks * T
    tiles = picks.shape[0]
    return pl.pallas_call(
        functools.partial(products_kernel, count, blocks, shares),
        grid_spec=pltpu.PrefetchScalarGridSpec(
            num_scalar_prefetch=1,
            grid=(),
            in_specs=[pl.BlockSpec(memory_space=pl.ANY)],
            out_specs=[pl.BlockSpec(memory_space=pl.ANY)] * shares,
            scratch_shapes=[
                pltpu.VMEM((ARRIVING, BATCH) + got.shape[1:], F32),
                pltpu.VMEM(((chunks + FIRST) * T, 2 * T), BF16),
                pltpu.VMEM((chunks + 8, T), jnp.int32),
                pltpu.SMEM((NAB + 1,), jnp.int32),
                pltpu.VMEM((FREQS, pairs, T), F32),
                pltpu.VMEM((pairs, T), F32),
                pltpu.VMEM((NAB, 2 * T, pairs), BF16),
                pltpu.VMEM((NAB, 2, pairs, FREQS * T), BF16),
                pltpu.VMEM((2, GROUP, FREQS, T, T), F32),
                pltpu.SemaphoreType.DMA((ARRIVING,)),
                pltpu.SemaphoreType.DMA((2,)),
            ],
        ),
        out_shape=[jax.ShapeDtypeStruct((tiles // shares, FREQS, T, T), F32)] * shares,
        compiler_params=pltpu.CompilerParams(vmem_limit_bytes=61 * MIB),
        name="products",
    )(picks.reshape(-1), got)


def layout(me, owner):
    plane = jnp.arange(16, dtype=jnp.int32)
    high, low = plane // 4, plane % 4
    here = jnp.where(owner == 0, me % 4, me // 32)
    lists = []
    for step in (2, 1, 3, 0):
        at = (here + step) % 4
        lists.append(
            jnp.where(owner == 0, ((high * 4 + low) * 2) * 4 + at, ((at * 4 + high) * 2 + 1) * 4 + low)
        )
    return lists


def shift(step):
    pairs = []
    for d in range(128):
        x, y, core, z = d // 32, d // 8 % 4, d // 4 % 2, d % 4
        if core == 0:
            z = (z + step) % 4
        else:
            x = (x + step) % 4
        pairs.append((d, ((x * 4 + y) * 2 + core) * 4 + z))
    return pairs


PLANES = [[(plane * 2) * 4 + z for plane in range(16)] for z in range(4)] + [
    [((x * 4 + plane // 4) * 2 + 1) * 4 + plane % 4 for plane in range(16)] for x in range(4)
]
SWAP = [(d, d ^ 4) for d in range(128)]


def on_device(b_tiles, tile_aux, tile_pair, freq_weights, kept):
    count = b_tiles.shape[0]
    devices = lax.axis_size("d")
    me = lax.axis_index("d")
    core = me // 4 % 2
    blocks = freq_weights.shape[1] // T

    sent = by_column(b_tiles, tile_aux, tile_pair, freq_weights, devices).reshape(devices, count + EXTRA, T)
    got = lax.all_to_all(sent, "d", split_axis=0, concat_axis=0, tiled=True)

    far, up, down, keep = zip(*[layout(me, owner) for owner in (1 - core, core)])
    picks = kept[jnp.concatenate(far + up + down + keep)]
    partial = products(picks, 8, got, count, blocks)
    far, up, down, keep = [(own, lax.ppermute(away, "d", SWAP)) for away, own in zip(partial[0::2], partial[1::2])]
    low, high = slice(0, 8), slice(8, 16)

    def both(pair, part):
        return pair[0][part] + pair[1][part]

    from_below = lax.ppermute(both(far, low), "d", shift(1))
    from_above = lax.ppermute(both(far, high), "d", shift(-1))
    up_high = lax.ppermute(both(up, high), "d", shift(1))
    down_low = lax.ppermute(both(down, low), "d", shift(-1))
    up_low = lax.ppermute(both(up, low) + from_below, "d", shift(1))
    down_high = lax.ppermute(both(down, high) + from_above, "d", shift(-1))
    summed = jnp.concatenate([both(keep, low) + up_low + down_low, both(keep, high) + up_high + down_high])
    parts = lax.all_to_all(summed, "d", split_axis=0, concat_axis=0, tiled=True, axis_index_groups=PLANES)
    return jnp.sum(parts, axis=0, keepdims=True)


def solution(mesh):
    flat = Mesh(mesh.devices.reshape(-1), ("d",))
    placed = (P("d", None, None), P("d"), P("d"), P(None, "d"), P())
    return jax.shard_map(
        on_device, mesh=flat, in_specs=placed, out_specs=P("d", None, None, None), check_vma=False
    )
```

time: 237 us -> 225 us (0.949)
  Pallas kernels: 85.2 us -> 71.7 us
  waiting for transfers between devices: 89 us -> 94.1 us
  other arithmetic: 8.29 us -> 4.76 us
    pallas_call x2 -> x1, Pallas kernels: 77.6 us -> 64 us  [products(): pl.pallas_call(functools.partial(products_kernel, count, blocks, shares),...]
    ppermute x7 -> x10, waiting for transfers between devices: 32.3 us -> 37.2 us  [the longest x1 11.5 us: on_device(): from_below = lax.ppermute(both(far, low), 'd', shift(1))]
    add x4, other arithmetic: 7.25 us -> 3.73 us  [the longest x2 2.39 us: both(): return pair[0][part] + pair[1][part]]
    ppermute x7 -> x10, starting transfers between devices: 7.87 us -> 8.03 us  [the longest x1 2.55 us: on_device(): from_above = lax.ppermute(both(far, high), 'd', shift(-1))]
  transfers between devices with their start and end apart: 8 -> 11, of which waited for: 5 -> 6; matrix products, arithmetic and copies ran while one was open for 1% -> 2% of each run, Pallas kernels for 12% -> 0%
where the time goes in v3:
time: 225 us
  waiting for transfers between devices  94.1 us (42%)
  Pallas kernels  71.7 us (32%)
  blocking collectives  31.2 us (14%)
  starting transfers between devices  19.9 us (9%)
  other arithmetic  4.76 us (2%)
  local copies, waits for them, and re-layouts  2.61 us (1%)
    pallas_call x1, Pallas kernels, products(): pl.pallas_call(functools.partial(products_kernel, count, blocks, shares),...  64 us
    all_to_all x1, waiting for transfers between devices, on_device(): got = lax.all_to_all(sent, 'd', split_axis=0, concat_axis=0, tiled=True)  56.9 us
    all_to_all x1, blocking collectives, on_device(): lax.all_to_all(summed, 'd', split_axis=0, concat_axis=0, tiled=True, axis...  31.2 us
    all_to_all x1, starting transfers between devices, on_device(): got = lax.all_to_all(sent, 'd', split_axis=0, concat_axis=0, tiled=True)  11.9 us
    ppermute x1, waiting for transfers between devices, on_device(): from_below = lax.ppermute(both(far, low), 'd', shift(1))  11.5 us
    ppermute x1, waiting for transfers between devices, on_device(): up_high = lax.ppermute(both(up, high), 'd', shift(1))  11.2 us
    ppermute x1, waiting for transfers between devices, on_device(): up_low = lax.ppermute(both(up, low) + from_below, 'd', shift(1))  10.5 us
    pallas_call x1, Pallas kernels, by_column(): pl.pallas_call(functools.partial(columns_kernel, groups, blocks, devices)...  7.7 us
  transfers between devices with their start and end apart: 11, of which 6 were waited for; matrix products, arithmetic and copies ran while one was open for 2% of the time, Pallas kernels for 0%

profile of v3, /device:TPU:1, one launch (start us, length us, event | category | flops | bytes accessed | tf_op | source)
XLA Modules:
  0.0 224.6 jit_solution(4773074334664098151)
XLA Ops:
  0.0 7.7 %columns.1 = f32[128,9,8,128]{3,2,1,0:T(8,128)} custom-call(f32[64,128,128]{2,1,0:T(8,128)} %tiles_ref.1, s32[1,64]{1,0:T(1,128)} %bitcast.23, s32[1,64]{1,0:T(1,128)} %bitcast.24, f32[2,1536]{1,0:T(2,128)} %weights_ref.1), custom_call_target="tpu_custom_call" | custom-call | tf_op jit(solution)/shard_map/columns/pallas_call | solution.py:50
  7.7 0.0 copy-start.3
  7.7 11.9 %all-to-all-start = ((f32[128,72,128]{2,1,0:T(8,128)}), f32[128,72,128]{2,1,0:T(8,128)}, u32[]{:S(2)}, u32[]{:S(2)}) async-start(f32[128,72,128]{2,1,0:T(8,128)} %bitcast.22), calls=%async_computation | async-start | bytes 9437184 | tf_op jit(solution)/shard_map/all_to_all | solution.py:297
  19.8 0.0 copy-done.3
  19.8 0.1 copy.7
  20.0 0.1 concatenate.49
  20.1 0.6 gather_fusion
  20.7 0.7 reshape.191.picks
  21.4 56.9 %all-to-all-done.got_ref = f32[128,72,128]{2,1,0:T(8,128)} async-done(((f32[128,72,128]{2,1,0:T(8,128)}), f32[128,72,128]{2,1,0:T(8,128)}, u32[]{:S(2)}, u32[]{:S(2)}) %all-to-all-start) | async-done | bytes 4718624 | tf_op jit(solution)/shard_map/all_to_all | solution.py:297
  78.3 64.0 %products.1 = (f32[16,2,128,128]{3,2,1,0:T(8,128)}, f32[16,2,128,128]{3,2,1,0:T(8,128)}, f32[16,2,128,128]{3,2,1,0:T(8,128)}, f32[16,2,128,128]{3,2,1,0:T(8,128)...) custom-call(s32[256]{0:T(256)} %reshape.191.picks, ...), custom_call_target="tpu_custom_call" | custom-call | tf_op jit(solution)/shard_map/products/pallas_call | solution.py:231
  142.4 0.6 collective-permute-start.2
  143.0 0.1 collective-permute-start.1
  143.1 0.4 collective-permute-start.5
  143.5 3.5 %collective-permute-done.2 = f32[16,2,128,128]{3,2,1,0:T(8,128)S(1)} collective-permute-done((f32[16,2,128,128]{3,2,1,0:T(8,128)}, f32[16,2,128,128]{3,2,1,0:T(8,128)S(1)}, u32[]{:S(2)}, u32[]{:S(2)}) %collective-permute-start.2) | collective-permute-done | bytes 2097184 | tf_op jit(solution)/shard_map/ppermute | solution.py:302
  147.0 0.0 copy-start.4
  147.0 0.0 copy-start.2
  147.0 2.0 slice_add_fusion.5
  149.0 0.2 collective-permute-start.3
  149.2 2.5 %collective-permute-start.8 = (f32[8,2,128,128]{3,2,1,0:T(8,128)S(1)}, f32[8,2,128,128]{3,2,1,0:T(8,128)S(1)}, u32[]{:S(2)}, u32[]{:S(2)}) collective-permute-start(f32[8,2,128,128]{3,2,1,0:T(8,128)S(1)} %get-tuple-element.26), channel_id=1, source_target_pairs={{0,3},{1,0},{2,1},{3,2},{4,100},{5,101},{6,102},{7,103},{8,11},{9,... | collective-permute-start | bytes 3145736 | tf_op jit(solution)/shard_map/ppermute | solution.py:309
  151.7 0.0 copy-done.4
  151.7 0.9 collective-permute-start
  152.7 0.0 collective-permute-done.1
  152.7 11.5 %collective-permute-done.3 = f32[8,2,128,128]{3,2,1,0:T(8,128)S(1)} collective-permute-done((f32[8,2,128,128]{3,2,1,0:T(8,128)S(1)}, f32[8,2,128,128]{3,2,1,0:T(8,128)S(1)}, u32[]{:S(2)}, u32[]{:S(2)}) %collective-permute-start.3) | collective-permute-done | bytes 1048608 | tf_op jit(solution)/shard_map/ppermute | solution.py:308
  164.2 0.0 copy-done.2
  164.2 0.0 copy-start.1
  164.2 0.4 fusion.3
  164.6 0.1 collective-permute-start.4
  164.7 0.1 collective-permute-start.7
  164.7 0.0 collective-permute-done.5
  164.8 0.0 collective-permute-done.8
  164.8 1.0 copy-done.1
  165.8 0.0 copy-start
  165.8 0.4 slice_add_fusion.4
  166.2 1.7 collective-permute-start.6
  167.9 1.4 collective-permute-start.9
  169.3 0.0 collective-permute-done
  169.3 10.5 %collective-permute-done.4 = f32[8,2,128,128]{3,2,1,0:T(8,128)S(1)} collective-permute-done((f32[8,2,128,128]{3,2,1,0:T(8,128)S(1)}, f32[8,2,128,128]{3,2,1,0:T(8,128)S(1)}, u32[]{:S(2)}, u32[]{:S(2)}) %collective-permute-start.4) | collective-permute-done | bytes 1048608 | tf_op jit(solution)/shard_map/ppermute | solution.py:312
  179.8 11.2 %collective-permute-done.7 = f32[8,2,128,128]{3,2,1,0:T(8,128)S(1)} collective-permute-done((f32[8,2,128,128]{3,2,1,0:T(8,128)S(1)}, f32[8,2,128,128]{3,2,1,0:T(8,128)S(1)}, u32[]{:S(2)}, u32[]{:S(2)}) %collective-permute-start.7) | collective-permute-done | bytes 1048608 | tf_op jit(solution)/shard_map/ppermute | solution.py:310
  191.0 0.0 collective-permute-done.6
  191.0 0.4 collective-permute-done.9
  191.5 0.0 copy-done
  191.5 1.0 fusion.5
  192.4 0.2 pad_maximum_fusion
  192.6 31.2 %all_to_all.10 = f32[16,2,128,128]{3,2,1,0:T(8,128)S(1)} all-to-all(f32[16,2,128,128]{3,2,1,0:T(8,128)S(1)} %pad_maximum_fusion), channel_id=1, replica_groups={{0,8,16,24,32,40,48,56,64,72,80,88,96,104,112,120},{1,9,17,25,33,41,49,..., dimensions={0} | all-to-all | bytes 4194304 | tf_op jit(solution)/shard_map/all_to_all | solution.py:315
  223.9 0.8 reduce_sum.9
  (6 shorter events, 0.1 us)
Async XLA Ops:
  7.7 12.1 %copy-start.3 = (s32[128,2]{0,1:T(2,128)S(1)}, s32[128,2]{0,1:T(2,128)}, u32[]{:S(2)}) copy-start(s32[128,2]{0,1:T(2,128)} %param.9) | copy-start | bytes 3076
  7.7 70.6 %all-to-all-start = ((f32[128,72,128]{2,1,0:T(8,128)}), f32[128,72,128]{2,1,0:T(8,128)}, u32[]{:S(2)}, u32[]{:S(2)}) async-start(f32[128,72,128]{2,1,0:T(8,128)} %bitcast.22), calls=%async_computation | async-start | bytes 9437184 | tf_op jit(solution)/shard_map/all_to_all | solution.py:297
  142.4 4.6 %collective-permute-start.2 = (f32[16,2,128,128]{3,2,1,0:T(8,128)}, f32[16,2,128,128]{3,2,1,0:T(8,128)S(1)}, u32[]{:S(2)}, u32[]{:S(2)}) collective-permute-start(f32[16,2,128,128]{3,2,1,0:T(8,128)} %get-tuple-element.18), channel_id=1, source_target_pairs={{0,4},{1,5},{2,6},{3,7},{4,0},{5,1},{6,2},{7,3},{8,12},{9,13},{10,... | collective-permute-start | bytes 6291464 | tf_op jit(solution)/shard_map/ppermute | solution.py:302
  143.0 9.7 %collective-permute-start.1 = (f32[16,2,128,128]{3,2,1,0:T(8,128)}, f32[16,2,128,128]{3,2,1,0:T(8,128)S(1)}, u32[]{:S(2)}, u32[]{:S(2)}) collective-permute-start(f32[16,2,128,128]{3,2,1,0:T(8,128)} %get-tuple-element.16), channel_id=1, source_target_pairs={{0,4},{1,5},{2,6},{3,7},{4,0},{5,1},{6,2},{7,3},{8,12},{9,13},{10,... | collective-permute-start | bytes 6291464 | tf_op jit(solution)/shard_map/ppermute | solution.py:302
  143.1 21.7 %collective-permute-start.5 = (f32[16,2,128,128]{3,2,1,0:T(8,128)}, f32[16,2,128,128]{3,2,1,0:T(8,128)S(1)}, u32[]{:S(2)}, u32[]{:S(2)}) collective-permute-start(f32[16,2,128,128]{3,2,1,0:T(8,128)} %get-tuple-element.20), channel_id=1, source_target_pairs={{0,4},{1,5},{2,6},{3,7},{4,0},{5,1},{6,2},{7,3},{8,12},{9,13},{10,... | collective-permute-start | bytes 6291464 | tf_op jit(solution)/shard_map/ppermute | solution.py:302
  147.0 4.7 %copy-start.4 = (f32[16,2,128,128]{3,2,1,0:T(8,128)S(1)}, f32[16,2,128,128]{3,2,1,0:T(8,128)}, u32[]{:S(2)}) copy-start(f32[16,2,128,128]{3,2,1,0:T(8,128)} %get-tuple-element.14) | copy-start | bytes 6291460
  147.0 17.2 %copy-start.2 = (f32[16,2,128,128]{3,2,1,0:T(8,128)S(1)}, f32[16,2,128,128]{3,2,1,0:T(8,128)}, u32[]{:S(2)}) copy-start(f32[16,2,128,128]{3,2,1,0:T(8,128)} %get-tuple-element.15) | copy-start | bytes 6291460
  149.0 15.2 %collective-permute-start.3 = (f32[8,2,128,128]{3,2,1,0:T(8,128)S(1)}, f32[8,2,128,128]{3,2,1,0:T(8,128)S(1)}, u32[]{:S(2)}, u32[]{:S(2)}) collective-permute-start(f32[8,2,128,128]{3,2,1,0:T(8,128)S(1)} %get-tuple-element.25), channel_id=1, source_target_pairs={{0,1},{1,2},{2,3},{3,0},{4,36},{5,37},{6,38},{7,39},{8,9},{9,10},{... | collective-permute-start | bytes 3145736 | tf_op jit(solution)/shard_map/ppermute | solution.py:308
  149.2 15.6 %collective-permute-start.8 = (f32[8,2,128,128]{3,2,1,0:T(8,128)S(1)}, f32[8,2,128,128]{3,2,1,0:T(8,128)S(1)}, u32[]{:S(2)}, u32[]{:S(2)}) collective-permute-start(f32[8,2,128,128]{3,2,1,0:T(8,128)S(1)} %get-tuple-element.26), channel_id=1, source_target_pairs={{0,3},{1,0},{2,1},{3,2},{4,100},{5,101},{6,102},{7,103},{8,11},{9,... | collective-permute-start | bytes 3145736 | tf_op jit(solution)/shard_map/ppermute | solution.py:309
  151.7 17.6 %collective-permute-start = (f32[16,2,128,128]{3,2,1,0:T(8,128)S(1)}, f32[16,2,128,128]{3,2,1,0:T(8,128)S(1)}, u32[]{:S(2)}, u32[]{:S(2)}) collective-permute-start(f32[16,2,128,128]{3,2,1,0:T(8,128)S(1)} %copy-done.4), channel_id=1, source_target_pairs={{0,4},{1,5},{2,6},{3,7},{4,0},{5,1},{6,2},{7,3},{8,12},{9,13},{10,... | collective-permute-start | bytes 6291464 | tf_op jit(solution)/shard_map/ppermute | solution.py:302
  164.2 1.6 copy-start.1
  164.6 15.2 %collective-permute-start.4 = (f32[8,2,128,128]{3,2,1,0:T(8,128)S(1)}, f32[8,2,128,128]{3,2,1,0:T(8,128)S(1)}, u32[]{:S(2)}, u32[]{:S(2)}) collective-permute-start(f32[8,2,128,128]{3,2,1,0:T(8,128)S(1)} %get-tuple-element.23), channel_id=1, source_target_pairs={{0,1},{1,2},{2,3},{3,0},{4,36},{5,37},{6,38},{7,39},{8,9},{9,10},{... | collective-permute-start | bytes 3145736 | tf_op jit(solution)/shard_map/ppermute | solution.py:312
  164.7 26.4 %collective-permute-start.7 = (f32[8,2,128,128]{3,2,1,0:T(8,128)S(1)}, f32[8,2,128,128]{3,2,1,0:T(8,128)S(1)}, u32[]{:S(2)}, u32[]{:S(2)}) collective-permute-start(f32[8,2,128,128]{3,2,1,0:T(8,128)S(1)} %get-tuple-element.24), channel_id=1, source_target_pairs={{0,1},{1,2},{2,3},{3,0},{4,36},{5,37},{6,38},{7,39},{8,9},{9,10},{... | collective-permute-start | bytes 3145736 | tf_op jit(solution)/shard_map/ppermute | solution.py:310
  165.8 25.7 %copy-start = (f32[16,2,128,128]{3,2,1,0:T(8,128)S(1)}, f32[16,2,128,128]{3,2,1,0:T(8,128)}, u32[]{:S(2)}) copy-start(f32[16,2,128,128]{3,2,1,0:T(8,128)} %get-tuple-element.13) | copy-start | bytes 6291460
  166.2 24.8 %collective-permute-start.6 = (f32[8,2,128,128]{3,2,1,0:T(8,128)S(1)}, f32[8,2,128,128]{3,2,1,0:T(8,128)S(1)}, u32[]{:S(2)}, u32[]{:S(2)}) collective-permute-start(f32[8,2,128,128]{3,2,1,0:T(8,128)S(1)} %get-tuple-element.27), channel_id=1, source_target_pairs={{0,3},{1,0},{2,1},{3,2},{4,100},{5,101},{6,102},{7,103},{8,11},{9,... | collective-permute-start | bytes 3145736 | tf_op jit(solution)/shard_map/ppermute | solution.py:311
  167.9 23.5 %collective-permute-start.9 = (f32[8,2,128,128]{3,2,1,0:T(8,128)S(1)}, f32[8,2,128,128]{3,2,1,0:T(8,128)S(1)}, u32[]{:S(2)}, u32[]{:S(2)}) collective-permute-start(f32[8,2,128,128]{3,2,1,0:T(8,128)S(1)} %get-tuple-element.28), channel_id=1, source_target_pairs={{0,3},{1,0},{2,1},{3,2},{4,100},{5,101},{6,102},{7,103},{8,11},{9,... | collective-permute-start | bytes 3145736 | tf_op jit(solution)/shard_map/ppermute | solution.py:313

commit v4 on v3

--- a/solution.py
+++ b/solution.py
@@ -16,7 +16,8 @@
 MIB = 1024 * 1024
 ARRIVING = 4
 BATCH = 16
-GROUP = 16
+KERNEL_MIB = 12
+GROUP = 8
 BF16 = jnp.bfloat16
 F32 = jnp.float32
 
@@ -62,7 +63,7 @@
     )(b_tiles, aux[None], pair[None], weights)
 
 
-def multiply(picks, left, right, stage, outs, out_sems):
+def multiply(begin, picks, left, right, stage, outs, out_sems):
     share = outs[0].shape[0]
 
     def copies(g):
@@ -78,8 +79,8 @@
             copies(g)[0].wait()
 
         for k in range(GROUP):
-            p = picks[2 * (g * GROUP + k)]
-            q = picks[2 * (g * GROUP + k) + 1]
+            p = picks[2 * (begin + g * GROUP + k)]
+            q = picks[2 * (begin + g * GROUP + k) + 1] - 1
             both = jnp.dot(left[p], right[q, 0], preferred_element_type=F32)
             small = jnp.dot(left[p, 0:T, :], right[q, 1], preferred_element_type=F32)
             result = both[0:T] + (both[T:] + small)
@@ -98,9 +99,9 @@
         copies(g)[0].wait()
 
 
-def products_kernel(count, blocks, shares, picks, got_ref, *refs):
+def first_kernel(count, blocks, shares, picks, got_ref, left, right, *refs):
     outs, (
-        got, rows, keys, starts, weight, total, left, right, stage,
+        got, rows, keys, starts, weight, total, stage,
         got_sems, out_sems,
     ) = refs[:shares], refs[shares:]
     pairs = blocks * T
@@ -163,17 +164,19 @@
     def put(a, n, value):
         at = slice(n * half, (n + 1) * half)
 
+        row = jnp.minimum(a, NAB - 2)
+        slot = jnp.maximum(a, 1) - 1
         turned = value.T
         hi = turned.astype(BF16)
         lo = (turned - hi.astype(F32)).astype(BF16)
-        left[a, 0:T, at] = hi
-        left[a, T:, at] = lo
+        left[row, 0:T, at] = hi
+        left[row, T:, at] = lo
         for f in range(FREQS):
             scaled = value * weight[f, at, :]
             hi = scaled.astype(BF16)
             cols = slice(f * T, (f + 1) * T)
-            right[a, 0, at, cols] = hi
-            right[a, 1, at, cols] = (scaled - hi.astype(F32)).astype(BF16)
+            right[slot, 0, at, cols] = hi
+            right[slot, 1, at, cols] = (scaled - hi.astype(F32)).astype(BF16)
 
     def straight(a):
         begin = starts[a]
@@ -190,51 +193,52 @@
             put(a, n, both[:, 0:T] + both[:, T:])
 
     def whole(a):
-        chunk = starts[a] // T
-        end = starts[a + 1]
-
-        @pl.when(end - (starts[a] // 16) * 16 > wide)
-        def _():
-            total[...] = jnp.zeros_like(total)
-
-            def add(s, carry):
-                key = keys[pl.ds(s, 1), :] - a * pairs
-                for n in range(pairs // half):
-                    hot = jnp.where(place[:, 0:T] == key - n * half, 1.0, 0.0).astype(BF16)
-                    both = jnp.dot(
-                        hot, rows[pl.ds(pl.multiple_of(s * T, T), T), :], preferred_element_type=F32
-                    )
-                    total[n * half : (n + 1) * half, :] += both[:, 0:T] + both[:, T:]
-                return carry
-
-            lax.fori_loop(chunk, (end + T - 1) // T, add, 0)
+        total[...] = jnp.zeros_like(total)
+
+        def add(s, carry):
+            key = keys[pl.ds(s, 1), :] - a * pairs
             for n in range(pairs // half):
-                put(a, n, total[n * half : (n + 1) * half, :])
+                hot = jnp.where(place[:, 0:T] == key - n * half, 1.0, 0.0).astype(BF16)
+                both = jnp.dot(hot, rows[pl.ds(pl.multiple_of(s * T, T), T), :], preferred_element_type=F32)
+                total[n * half : (n + 1) * half, :] += both[:, 0:T] + both[:, T:]
+            return carry
+
+        lax.fori_loop(starts[a] // T, (starts[a + 1] + T - 1) // T, add, 0)
+        for n in range(pairs // half):
+            put(a, n, total[n * half : (n + 1) * half, :])
+
+    def beyond(a):
+        return starts[a + 1] - (starts[a] // 16) * 16 > wide
 
     def columns(i, carry):
-        pair = 2 * i, 2 * i + 1
+        last = 2 * i == NAB - 2
+        pair = jnp.where(last, NAB - 1, 2 * i), jnp.where(last, NAB - 2, 2 * i + 1)
         for a in pair:
             straight(a)
-        for a in pair:
-            whole(a)
+
+        @pl.when(jnp.logical_or(beyond(pair[0]), beyond(pair[1])))
+        def _():
+            for a in pair:
+                whole(a)
+
         return carry
 
     lax.fori_loop(0, NAB // 2, columns, 0)
-    multiply(picks, left, right, stage, outs, out_sems)
-
-
-def products(picks, shares, got, count, blocks):
+    multiply(0, picks, left, right, stage, outs, out_sems)
+
+
+def first_products(picks, tiles, got, count, blocks):
     sources = got.shape[0]
     chunks = sources * count // T
     pairs = blocks * T
-    tiles = picks.shape[0]
+    shares = 2
     return pl.pallas_call(
-        functools.partial(products_kernel, count, blocks, shares),
+        functools.partial(first_kernel, count, blocks, shares),
         grid_spec=pltpu.PrefetchScalarGridSpec(
             num_scalar_prefetch=1,
             grid=(),
             in_specs=[pl.BlockSpec(memory_space=pl.ANY)],
-            out_specs=[pl.BlockSpec(memory_space=pl.ANY)] * shares,
+            out_specs=[pl.BlockSpec(memory_space=pltpu.VMEM)] * 2 + [pl.BlockSpec(memory_space=pl.ANY)] * shares,
             scratch_shapes=[
                 pltpu.VMEM((ARRIVING, BATCH) + got.shape[1:], F32),
                 pltpu.VMEM(((chunks + FIRST) * T, 2 * T), BF16),
@@ -242,17 +246,74 @@
                 pltpu.SMEM((NAB + 1,), jnp.int32),
                 pltpu.VMEM((FREQS, pairs, T), F32),
                 pltpu.VMEM((pairs, T), F32),
-                pltpu.VMEM((NAB, 2 * T, pairs), BF16),
-                pltpu.VMEM((NAB, 2, pairs, FREQS * T), BF16),
                 pltpu.VMEM((2, GROUP, FREQS, T, T), F32),
                 pltpu.SemaphoreType.DMA((ARRIVING,)),
                 pltpu.SemaphoreType.DMA((2,)),
             ],
         ),
-        out_shape=[jax.ShapeDtypeStruct((tiles // shares, FREQS, T, T), F32)] * shares,
-        compiler_params=pltpu.CompilerParams(vmem_limit_bytes=61 * MIB),
-        name="products",
-    )(picks.reshape(-1), got)
+        out_shape=[
+            pltpu.VMEM((NAB - 1, 2 * T, pairs), BF16),
+            pltpu.VMEM((NAB - 1, 2, pairs, FREQS * T), BF16),
+        ]
+        + [jax.ShapeDtypeStruct((tiles // shares, FREQS, T, T), F32)] * shares,
+        compiler_params=pltpu.CompilerParams(vmem_limit_bytes=KERNEL_MIB * MIB),
+        name="first_products",
+    )(picks, got)
+
+
+def more_kernel(at, fences, picks, left, right, *refs):
+    outs, (stage, out_sems) = refs[fences:-2], refs[-2:]
+    multiply(at, picks, left, right, stage, outs, out_sems)
+
+
+def more_products(at, picks, left, right, fence=()):
+    return pl.pallas_call(
+        functools.partial(more_kernel, at, len(fence)),
+        grid_spec=pltpu.PrefetchScalarGridSpec(
+            num_scalar_prefetch=1,
+            grid=(),
+            in_specs=[pl.BlockSpec(memory_space=pltpu.VMEM)] * 2
+            + [pl.BlockSpec(memory_space=pl.ANY)] * len(fence),
+            out_specs=[pl.BlockSpec(memory_space=pl.ANY)] * 2,
+            scratch_shapes=[
+                pltpu.VMEM((2, GROUP, FREQS, T, T), F32),
+                pltpu.SemaphoreType.DMA((2,)),
+            ],
+        ),
+        out_shape=[jax.ShapeDtypeStruct((16, FREQS, T, T), F32)] * 2,
+        compiler_params=pltpu.CompilerParams(vmem_limit_bytes=KERNEL_MIB * MIB),
+        cost_estimate=pl.CostEstimate(
+            flops=12 * GROUP * FREQS * T * T * left.shape[2], bytes_accessed=4 * MIB, transcendentals=0
+        ),
+        name="more_products",
+    )(
+        picks,
+        pltpu.with_memory_space_constraint(left, pltpu.VMEM),
+        pltpu.with_memory_space_constraint(right, pltpu.VMEM),
+        *fence,
+    )
+
+
+def add_kernel(a_low, a_high, b_low, b_high, low, high):
+    low[...] = a_low[...] + b_low[...]
+    high[...] = a_high[...] + b_high[...]
+
+
+def add_halves(a, b):
+    half = a.shape[0] // 2
+    step = 2
+    block = (step,) + a.shape[1:]
+    first = pl.BlockSpec(block, lambda i: (i, 0, 0, 0))
+    second = pl.BlockSpec(block, lambda i: (i + half // step, 0, 0, 0))
+    return pl.pallas_call(
+        add_kernel,
+        grid=(half // step,),
+        in_specs=[first, second, first, second],
+        out_specs=[first, first],
+        out_shape=[jax.ShapeDtypeStruct((half,) + a.shape[1:], F32)] * 2,
+        compiler_params=pltpu.CompilerParams(vmem_limit_bytes=KERNEL_MIB * MIB),
+        name="add_halves",
+    )(a, a, b, b)
 
 
 def layout(me, owner):
@@ -297,21 +358,46 @@
     got = lax.all_to_all(sent, "d", split_axis=0, concat_axis=0, tiled=True)
 
     far, up, down, keep = zip(*[layout(me, owner) for owner in (1 - core, core)])
-    picks = kept[jnp.concatenate(far + up + down + keep)]
-    partial = products(picks, 8, got, count, blocks)
-    far, up, down, keep = [(own, lax.ppermute(away, "d", SWAP)) for away, own in zip(partial[0::2], partial[1::2])]
     low, high = slice(0, 8), slice(8, 16)
-
-    def both(pair, part):
-        return pair[0][part] + pair[1][part]
-
-    from_below = lax.ppermute(both(far, low), "d", shift(1))
-    from_above = lax.ppermute(both(far, high), "d", shift(-1))
-    up_high = lax.ppermute(both(up, high), "d", shift(1))
-    down_low = lax.ppermute(both(down, low), "d", shift(-1))
-    up_low = lax.ppermute(both(up, low) + from_below, "d", shift(1))
-    down_high = lax.ppermute(both(down, high) + from_above, "d", shift(-1))
-    summed = jnp.concatenate([both(keep, low) + up_low + down_low, both(keep, high) + up_high + down_high])
+    lists = [
+        [far[0], far[1]],
+        [up[0][high], down[0][low], up[1][high], down[1][low]],
+        [up[0][low], down[0][high], up[1][low], down[1][high]],
+        [keep[0], keep[1]],
+    ]
+    picks = kept[jnp.concatenate([part for some in lists for part in some])].reshape(-1)
+
+    def swap(tiles):
+        return lax.ppermute(tiles, "d", SWAP)
+
+    def send(pair):
+        return [lax.ppermute(part, "d", shift(step)) for part, step in zip(pair, (1, -1))]
+
+    left, right, away, far = first_products(picks, 32, got, count, blocks)
+    landed = swap(away)
+    away, second = more_products(32, picks, left, right)
+    away, landed = lax.optimization_barrier((away, landed))
+
+    leaving = add_halves(far, landed)
+    passing = send(leaving)
+    landed = swap(away)
+    away, third = more_products(64, picks, left, right, leaving)
+    away, landed, passing = lax.optimization_barrier((away, landed, passing))
+
+    leaving = add_halves(second, landed)
+    arrived = send(leaving)
+    landed = swap(away)
+    away, keep = more_products(96, picks, left, right, leaving)
+    away, landed, arrived = lax.optimization_barrier((away, landed, arrived))
+
+    last = send([third[low] + landed[low] + passing[0], third[high] + landed[high] + passing[1]])
+    landed = swap(away)
+    summed = jnp.concatenate(
+        [
+            keep[low] + landed[low] + last[0] + arrived[1],
+            keep[high] + landed[high] + last[1] + arrived[0],
+        ]
+    )
     parts = lax.all_to_all(summed, "d", split_axis=0, concat_axis=0, tiled=True, axis_index_groups=PLANES)
     return jnp.sum(parts, axis=0, keepdims=True)
 

time: 225 us -> 219 us (0.973)
  waiting for transfers between devices: 94.1 us -> 69.1 us
  local copies, waits for them, and re-layouts: 2.61 us -> 13.3 us
  Pallas kernels: 71.7 us -> 78.3 us
  starting transfers between devices: 19.9 us -> 22.5 us
    ppermute x10, waiting for transfers between devices: 37.2 us -> 12.5 us  [the longest x6 12.5 us: send(): lax.ppermute(part, 'd', shift(step))]
    unnamed x11 -> x27, local copies, waits for them, and re-layouts: 1.15 us -> 11.6 us
    pallas_call x1 -> x6, Pallas kernels: 64 us -> 70.6 us  [the longest x3 36.7 us: more_products(): pl.pallas_call(functools.partial(more_kernel, at, len(fence)), grid_spec=...]
    ppermute x10, starting transfers between devices: 8.03 us -> 10.6 us  [the longest x6 8.24 us: send(): lax.ppermute(part, 'd', shift(step))]
  transfers between devices with their start and end apart: 11 -> 11, of which waited for: 6 -> 2; matrix products, arithmetic and copies ran while one was open for 2% -> 2% of each run, Pallas kernels for 0% -> 17%
where the time goes in v4:
time: 219 us
  Pallas kernels  78.3 us (36%)
  waiting for transfers between devices  69.1 us (32%)
  blocking collectives  31.2 us (14%)
  starting transfers between devices  22.5 us (10%)
  local copies, waits for them, and re-layouts  13.3 us (6%)
  other arithmetic  3.85 us (2%)
    all_to_all x1, waiting for transfers between devices, on_device(): got = lax.all_to_all(sent, 'd', split_axis=0, concat_axis=0, tiled=True)  56.6 us
    pallas_call x3, Pallas kernels, more_products(): pl.pallas_call(functools.partial(more_kernel, at, len(fence)), grid_spec=...  36.7 us
    pallas_call x1, Pallas kernels, first_products(): pl.pallas_call(functools.partial(first_kernel, count, blocks, shares), gr...  33.3 us
    all_to_all x1, blocking collectives, on_device(): lax.all_to_all(summed, 'd', split_axis=0, concat_axis=0, tiled=True, axis...  31.2 us
    ppermute x6, waiting for transfers between devices, send(): lax.ppermute(part, 'd', shift(step))  12.5 us
    all_to_all x1, starting transfers between devices, on_device(): got = lax.all_to_all(sent, 'd', split_axis=0, concat_axis=0, tiled=True)  11.9 us
    unnamed x27, local copies, waits for them, and re-layouts  11.6 us
    ppermute x6, starting transfers between devices, send(): lax.ppermute(part, 'd', shift(step))  8.24 us
  transfers between devices with their start and end apart: 11, of which 2 were waited for; matrix products, arithmetic and copies ran while one was open for 2% of the time, Pallas kernels for 17%

profile of v4, /device:TPU:1, one launch (start us, length us, event | category | flops | bytes accessed | tf_op | source)
XLA Modules:
  0.0 218.7 jit_solution(14639947822604951278)
XLA Ops:
  0.0 7.7 %columns.1 = f32[128,9,8,128]{3,2,1,0:T(8,128)} custom-call(f32[64,128,128]{2,1,0:T(8,128)} %tiles_ref.1, s32[1,64]{1,0:T(1,128)} %bitcast.31, s32[1,64]{1,0:T(1,128)} %bitcast.32, f32[2,1536]{1,0:T(2,128)} %weights_ref.1), custom_call_target="tpu_custom_call" | custom-call | tf_op jit(solution)/shard_map/columns/pallas_call | solution.py:51
  7.7 11.9 %all-to-all-start = ((f32[128,72,128]{2,1,0:T(8,128)}), f32[128,72,128]{2,1,0:T(8,128)}, u32[]{:S(2)}, u32[]{:S(2)}) async-start(f32[128,72,128]{2,1,0:T(8,128)} %bitcast.30), calls=%async_computation | async-start | bytes 9437184 | tf_op jit(solution)/shard_map/all_to_all | solution.py:358
  19.8 0.1 copy.7
  20.0 0.1 slice_bitcast_fusion.2
  20.1 0.1 slice_bitcast_fusion
  20.1 0.1 slice_bitcast_fusion.3
  20.2 0.1 slice_bitcast_fusion.1
  20.3 0.1 concatenate.61
  20.4 0.6 gather_fusion
  21.1 0.7 reshape.399.picks
  21.8 56.6 %all-to-all-done.got_ref = f32[128,72,128]{2,1,0:T(8,128)} async-done(((f32[128,72,128]{2,1,0:T(8,128)}), f32[128,72,128]{2,1,0:T(8,128)}, u32[]{:S(2)}, u32[]{:S(2)}) %all-to-all-start) | async-done | bytes 4718624 | tf_op jit(solution)/shard_map/all_to_all | solution.py:358
  78.4 33.3 %first_products.1 = (bf16[19,256,1536]{2,1,0:T(8,128)(2,1)S(1)}, bf16[19,2,1536,256]{3,2,1,0:T(8,128)(2,1)S(1)}, f32[16,2,128,128]{3,2,1,0:T(8,128)}, f32[16,2,128,128]{3,2,1,0:T(8,128)}) custom-call(s32[256]{0:T(256)} %reshape.399.picks, f32[128,72,128]{2,1,0:T(8,128)} %all-to-all-done.got_ref), custom_call_target="tpu_custom_call" | custom-call | tf_op jit(solution)/shard_map/first_products/pallas_call | solution.py:235
  111.7 0.6 collective-permute-start
  112.3 12.3 %more_products.3 = (f32[16,2,128,128]{3,2,1,0:T(8,128)}, f32[16,2,128,128]{3,2,1,0:T(8,128)}) custom-call(s32[256]{0:T(256)} %reshape.399.picks, bf16[19,256,1536]{2,1,0:T(8,128)(2,1)S(1)} %get-tuple-element.29.left, bf16[19,2,1536,256]{3,2,1,0:T(8,128)(2,1)S(1)} %get-tuple-element.30.right), custom_call_target="tpu_custom_call" | custom-call | flops 4831838208 | bytes 4194304 | tf_op jit(solution)/shard_map/more_products/pallas_call | solution.py:270
  124.6 0.0 collective-permute-done.b_low.b_high
  124.6 0.1 collective-permute-start.1
  124.7 0.3 add_halves.2
  125.0 0.2 collective-permute-start.2
  125.2 2.5 %collective-permute-start.3 = (f32[8,2,128,128]{3,2,1,0:T(8,128)S(1)}, f32[8,2,128,128]{3,2,1,0:T(8,128)S(1)}, u32[]{:S(2)}, u32[]{:S(2)}) collective-permute-start(f32[8,2,128,128]{3,2,1,0:T(8,128)S(1)} %get-tuple-element.37.refs_1_), channel_id=1, source_target_pairs={{0,3},{1,0},{2,1},{3,2},{4,100},{5,101},{6,102},{7,103},{8,11},{9,... | collective-permute-start | bytes 3145736 | tf_op jit(solution)/shard_map/ppermute | solution.py:374
  127.7 5.2 %copy-done.1 = bf16[19,256,1536]{2,1,0:T(8,128)(2,1)S(1)} copy-done((bf16[19,256,1536]{2,1,0:T(8,128)(2,1)S(1)}, bf16[19,256,1536]{2,1,0:T(8,128)(2,1)}, u32[]{:S(2)}) %copy-start.1) | copy-done | bytes 14942232
  133.0 12.2 %more_products.4 = (f32[16,2,128,128]{3,2,1,0:T(8,128)}, f32[16,2,128,128]{3,2,1,0:T(8,128)}) custom-call(s32[256]{0:T(256)} %reshape.399.picks, bf16[19,256,1536]{2,1,0:T(8,128)(2,1)S(1)} %copy-done.1, bf16[19,2,1536,256]{3,2,1,0:T(8,128)(2,1)S(1)} %get-tuple-element.30.right, f32[8,2,128,128]{3,2,1,0:T(8,128)} %copy-done.8, f32[8,2,128,128]{3,2,1,0:T(8,128)} %copy-done.6), custom_call_target="tpu_custom_call" | custom-call | flops 4831838208 | bytes 4194304 | tf_op jit(solution)/shard_map/more_products/pallas_call | solution.py:270
  145.2 0.0 collective-permute-done.2
  145.2 0.0 collective-permute-done.3
  145.3 0.0 collective-permute-done.1.b_low.b_high
  145.3 0.9 copy-done.11
  146.2 1.0 collective-permute-start.4
  147.2 0.3 add_halves.3
  147.5 0.0 copy-start.5
  147.5 0.0 copy-start.7
  147.5 0.2 collective-permute-start.5
  147.7 2.5 %collective-permute-start.6 = (f32[8,2,128,128]{3,2,1,0:T(8,128)S(1)}, f32[8,2,128,128]{3,2,1,0:T(8,128)S(1)}, u32[]{:S(2)}, u32[]{:S(2)}) collective-permute-start(f32[8,2,128,128]{3,2,1,0:T(8,128)S(1)} %get-tuple-element.42.refs_1_), channel_id=1, source_target_pairs={{0,3},{1,0},{2,1},{3,2},{4,100},{5,101},{6,102},{7,103},{8,11},{9,... | collective-permute-start | bytes 3145736 | tf_op jit(solution)/shard_map/ppermute | solution.py:374
  150.3 0.0 copy-done.5
  150.3 5.2 %copy-done.2 = bf16[19,256,1536]{2,1,0:T(8,128)(2,1)S(1)} copy-done((bf16[19,256,1536]{2,1,0:T(8,128)(2,1)S(1)}, bf16[19,256,1536]{2,1,0:T(8,128)(2,1)}, u32[]{:S(2)}) %copy-start.2) | copy-done | bytes 14942232
  155.5 12.2 %more_products.5 = (f32[16,2,128,128]{3,2,1,0:T(8,128)}, f32[16,2,128,128]{3,2,1,0:T(8,128)}) custom-call(s32[256]{0:T(256)} %reshape.399.picks, bf16[19,256,1536]{2,1,0:T(8,128)(2,1)S(1)} %copy-done.2, bf16[19,2,1536,256]{3,2,1,0:T(8,128)(2,1)S(1)} %get-tuple-element.30.right, f32[8,2,128,128]{3,2,1,0:T(8,128)} %copy-done.7, f32[8,2,128,128]{3,2,1,0:T(8,128)} %copy-done.5), custom_call_target="tpu_custom_call" | custom-call | flops 4831838208 | bytes 4194304 | tf_op jit(solution)/shard_map/more_products/pallas_call | solution.py:270
  167.8 0.0 collective-permute-done.5
  167.8 0.0 collective-permute-done.6
  167.8 0.0 collective-permute-done.4
  167.8 0.6 collective-permute-start.7
  168.5 1.9 add_add_fusion.1
  170.4 0.2 collective-permute-start.8
  170.6 2.5 %collective-permute-start.9 = (f32[8,2,128,128]{3,2,1,0:T(8,128)S(1)}, f32[8,2,128,128]{3,2,1,0:T(8,128)S(1)}, u32[]{:S(2)}, u32[]{:S(2)}) collective-permute-start(f32[8,2,128,128]{3,2,1,0:T(8,128)S(1)} %get-tuple-element.56), channel_id=1, source_target_pairs={{0,3},{1,0},{2,1},{3,2},{4,100},{5,101},{6,102},{7,103},{8,11},{9,... | collective-permute-start | bytes 3145736 | tf_op jit(solution)/shard_map/ppermute | solution.py:374
  173.2 12.5 %collective-permute-done.8 = f32[8,2,128,128]{3,2,1,0:T(8,128)S(1)} collective-permute-done((f32[8,2,128,128]{3,2,1,0:T(8,128)S(1)}, f32[8,2,128,128]{3,2,1,0:T(8,128)S(1)}, u32[]{:S(2)}, u32[]{:S(2)}) %collective-permute-start.8) | collective-permute-done | bytes 1048608 | tf_op jit(solution)/shard_map/ppermute | solution.py:374
  185.6 0.0 collective-permute-done.9
  185.6 0.0 collective-permute-done.7
  185.6 0.9 fusion.3
  186.5 0.2 pad_maximum_fusion
  186.7 31.2 %all_to_all.10 = f32[16,2,128,128]{3,2,1,0:T(8,128)S(1)} all-to-all(f32[16,2,128,128]{3,2,1,0:T(8,128)S(1)} %pad_maximum_fusion), channel_id=1, replica_groups={{0,8,16,24,32,40,48,56,64,72,80,88,96,104,112,120},{1,9,17,25,33,41,49,..., dimensions={0} | all-to-all | bytes 4194304 | tf_op jit(solution)/shard_map/all_to_all | solution.py:401
  218.0 0.8 reduce_sum.9
  (26 shorter events, 0.1 us)
Async XLA Ops:
  7.7 12.1 %copy-start.12 = (s32[128,2]{0,1:T(2,128)S(1)}, s32[128,2]{0,1:T(2,128)}, u32[]{:S(2)}) copy-start(s32[128,2]{0,1:T(2,128)} %param.9) | copy-start | bytes 3076
  7.7 70.6 %all-to-all-start = ((f32[128,72,128]{2,1,0:T(8,128)}), f32[128,72,128]{2,1,0:T(8,128)}, u32[]{:S(2)}, u32[]{:S(2)}) async-start(f32[128,72,128]{2,1,0:T(8,128)} %bitcast.30), calls=%async_computation | async-start | bytes 9437184 | tf_op jit(solution)/shard_map/all_to_all | solution.py:358
  111.7 12.9 %copy-start = (bf16[19,256,1536]{2,1,0:T(8,128)(2,1)}, bf16[19,256,1536]{2,1,0:T(8,128)(2,1)S(1)}, u32[]{:S(2)}) copy-start(bf16[19,256,1536]{2,1,0:T(8,128)(2,1)S(1)} %get-tuple-element.29.left) | copy-start | bytes 44826628
  111.7 12.9 %collective-permute-start = (f32[16,2,128,128]{3,2,1,0:T(8,128)}, f32[16,2,128,128]{3,2,1,0:T(8,128)S(1)}, u32[]{:S(2)}, u32[]{:S(2)}) collective-permute-start(f32[16,2,128,128]{3,2,1,0:T(8,128)} %get-tuple-element.34), channel_id=1, source_target_pairs={{0,4},{1,5},{2,6},{3,7},{4,0},{5,1},{6,2},{7,3},{8,12},{9,13},{10,... | collective-permute-start | bytes 6291464 | tf_op jit(solution)/shard_map/ppermute | solution.py:371
  112.3 12.4 %copy-start.4 = (f32[16,2,128,128]{3,2,1,0:T(8,128)S(1)}, f32[16,2,128,128]{3,2,1,0:T(8,128)}, u32[]{:S(2)}) copy-start(f32[16,2,128,128]{3,2,1,0:T(8,128)} %get-tuple-element.32.a_low.a_high) | copy-start | bytes 6291460
  124.6 20.7 %collective-permute-start.1 = (f32[16,2,128,128]{3,2,1,0:T(8,128)}, f32[16,2,128,128]{3,2,1,0:T(8,128)S(1)}, u32[]{:S(2)}, u32[]{:S(2)}) collective-permute-start(f32[16,2,128,128]{3,2,1,0:T(8,128)} %get-tuple-element.39), channel_id=1, source_target_pairs={{0,4},{1,5},{2,6},{3,7},{4,0},{5,1},{6,2},{7,3},{8,12},{9,13},{10,... | collective-permute-start | bytes 6291464 | tf_op jit(solution)/shard_map/ppermute | solution.py:371
  125.0 2.8 %copy-start.6 = (f32[8,2,128,128]{3,2,1,0:T(8,128)}, f32[8,2,128,128]{3,2,1,0:T(8,128)S(1)}, u32[]{:S(2)}) copy-start(f32[8,2,128,128]{3,2,1,0:T(8,128)S(1)} %get-tuple-element.37.refs_1_) | copy-start | bytes 3145732
  125.0 2.8 %copy-start.8 = (f32[8,2,128,128]{3,2,1,0:T(8,128)}, f32[8,2,128,128]{3,2,1,0:T(8,128)S(1)}, u32[]{:S(2)}) copy-start(f32[8,2,128,128]{3,2,1,0:T(8,128)S(1)} %get-tuple-element.36.refs_0_) | copy-start | bytes 3145732
  125.0 20.2 %collective-permute-start.2 = (f32[8,2,128,128]{3,2,1,0:T(8,128)S(1)}, f32[8,2,128,128]{3,2,1,0:T(8,128)S(1)}, u32[]{:S(2)}, u32[]{:S(2)}) collective-permute-start(f32[8,2,128,128]{3,2,1,0:T(8,128)S(1)} %get-tuple-element.36.refs_0_), channel_id=1, source_target_pairs={{0,1},{1,2},{2,3},{3,0},{4,36},{5,37},{6,38},{7,39},{8,9},{9,10},{... | collective-permute-start | bytes 3145736 | tf_op jit(solution)/shard_map/ppermute | solution.py:374
  125.2 20.0 %collective-permute-start.3 = (f32[8,2,128,128]{3,2,1,0:T(8,128)S(1)}, f32[8,2,128,128]{3,2,1,0:T(8,128)S(1)}, u32[]{:S(2)}, u32[]{:S(2)}) collective-permute-start(f32[8,2,128,128]{3,2,1,0:T(8,128)S(1)} %get-tuple-element.37.refs_1_), channel_id=1, source_target_pairs={{0,3},{1,0},{2,1},{3,2},{4,100},{5,101},{6,102},{7,103},{8,11},{9,... | collective-permute-start | bytes 3145736 | tf_op jit(solution)/shard_map/ppermute | solution.py:374
  127.7 5.2 %copy-start.1 = (bf16[19,256,1536]{2,1,0:T(8,128)(2,1)S(1)}, bf16[19,256,1536]{2,1,0:T(8,128)(2,1)}, u32[]{:S(2)}) copy-start(bf16[19,256,1536]{2,1,0:T(8,128)(2,1)} %copy-done) | copy-start | bytes 44826628
  133.0 14.2 %copy-start.3 = (f32[16,2,128,128]{3,2,1,0:T(8,128)S(1)}, f32[16,2,128,128]{3,2,1,0:T(8,128)}, u32[]{:S(2)}) copy-start(f32[16,2,128,128]{3,2,1,0:T(8,128)} %get-tuple-element.31.a_low.a_high) | copy-start | bytes 6291460
  145.3 1.0 copy-start.11
  146.2 21.6 %collective-permute-start.4 = (f32[16,2,128,128]{3,2,1,0:T(8,128)}, f32[16,2,128,128]{3,2,1,0:T(8,128)S(1)}, u32[]{:S(2)}, u32[]{:S(2)}) collective-permute-start(f32[16,2,128,128]{3,2,1,0:T(8,128)} %get-tuple-element.45), channel_id=1, source_target_pairs={{0,4},{1,5},{2,6},{3,7},{4,0},{5,1},{6,2},{7,3},{8,12},{9,13},{10,... | collective-permute-start | bytes 6291464 | tf_op jit(solution)/shard_map/ppermute | solution.py:371
  147.5 2.8 %copy-start.5 = (f32[8,2,128,128]{3,2,1,0:T(8,128)}, f32[8,2,128,128]{3,2,1,0:T(8,128)S(1)}, u32[]{:S(2)}) copy-start(f32[8,2,128,128]{3,2,1,0:T(8,128)S(1)} %get-tuple-element.42.refs_1_) | copy-start | bytes 3145732
  147.5 2.8 %copy-start.7 = (f32[8,2,128,128]{3,2,1,0:T(8,128)}, f32[8,2,128,128]{3,2,1,0:T(8,128)S(1)}, u32[]{:S(2)}) copy-start(f32[8,2,128,128]{3,2,1,0:T(8,128)S(1)} %get-tuple-element.41.refs_0_) | copy-start | bytes 3145732
  147.5 20.2 %collective-permute-start.5 = (f32[8,2,128,128]{3,2,1,0:T(8,128)S(1)}, f32[8,2,128,128]{3,2,1,0:T(8,128)S(1)}, u32[]{:S(2)}, u32[]{:S(2)}) collective-permute-start(f32[8,2,128,128]{3,2,1,0:T(8,128)S(1)} %get-tuple-element.41.refs_0_), channel_id=1, source_target_pairs={{0,1},{1,2},{2,3},{3,0},{4,36},{5,37},{6,38},{7,39},{8,9},{9,10},{... | collective-permute-start | bytes 3145736 | tf_op jit(solution)/shard_map/ppermute | solution.py:374
  147.7 20.1 %collective-permute-start.6 = (f32[8,2,128,128]{3,2,1,0:T(8,128)S(1)}, f32[8,2,128,128]{3,2,1,0:T(8,128)S(1)}, u32[]{:S(2)}, u32[]{:S(2)}) collective-permute-start(f32[8,2,128,128]{3,2,1,0:T(8,128)S(1)} %get-tuple-element.42.refs_1_), channel_id=1, source_target_pairs={{0,3},{1,0},{2,1},{3,2},{4,100},{5,101},{6,102},{7,103},{8,11},{9,... | collective-permute-start | bytes 3145736 | tf_op jit(solution)/shard_map/ppermute | solution.py:374
  150.3 5.2 %copy-start.2 = (bf16[19,256,1536]{2,1,0:T(8,128)(2,1)S(1)}, bf16[19,256,1536]{2,1,0:T(8,128)(2,1)}, u32[]{:S(2)}) copy-start(bf16[19,256,1536]{2,1,0:T(8,128)(2,1)} %copy-done) | copy-start | bytes 44826628
  155.5 12.9 %copy-start.10 = (f32[16,2,128,128]{3,2,1,0:T(8,128)S(1)}, f32[16,2,128,128]{3,2,1,0:T(8,128)}, u32[]{:S(2)}) copy-start(f32[16,2,128,128]{3,2,1,0:T(8,128)} %get-tuple-element.47) | copy-start | bytes 6291460
  167.8 17.8 %collective-permute-start.7 = (f32[16,2,128,128]{3,2,1,0:T(8,128)}, f32[16,2,128,128]{3,2,1,0:T(8,128)S(1)}, u32[]{:S(2)}, u32[]{:S(2)}) collective-permute-start(f32[16,2,128,128]{3,2,1,0:T(8,128)} %get-tuple-element.46), channel_id=1, source_target_pairs={{0,4},{1,5},{2,6},{3,7},{4,0},{5,1},{6,2},{7,3},{8,12},{9,13},{10,... | collective-permute-start | bytes 6291464 | tf_op jit(solution)/shard_map/ppermute | solution.py:371
  168.5 17.2 %copy-start.9 = (f32[16,2,128,128]{3,2,1,0:T(8,128)S(1)}, f32[16,2,128,128]{3,2,1,0:T(8,128)}, u32[]{:S(2)}) copy-start(f32[16,2,128,128]{3,2,1,0:T(8,128)} %get-tuple-element.43) | copy-start | bytes 6291460
  170.4 15.2 %collective-permute-start.8 = (f32[8,2,128,128]{3,2,1,0:T(8,128)S(1)}, f32[8,2,128,128]{3,2,1,0:T(8,128)S(1)}, u32[]{:S(2)}, u32[]{:S(2)}) collective-permute-start(f32[8,2,128,128]{3,2,1,0:T(8,128)S(1)} %get-tuple-element.55), channel_id=1, source_target_pairs={{0,1},{1,2},{2,3},{3,0},{4,36},{5,37},{6,38},{7,39},{8,9},{9,10},{... | collective-permute-start | bytes 3145736 | tf_op jit(solution)/shard_map/ppermute | solution.py:374
  170.6 15.0 %collective-permute-start.9 = (f32[8,2,128,128]{3,2,1,0:T(8,128)S(1)}, f32[8,2,128,128]{3,2,1,0:T(8,128)S(1)}, u32[]{:S(2)}, u32[]{:S(2)}) collective-permute-start(f32[8,2,128,128]{3,2,1,0:T(8,128)S(1)} %get-tuple-element.56), channel_id=1, source_target_pairs={{0,3},{1,0},{2,1},{3,2},{4,100},{5,101},{6,102},{7,103},{8,11},{9,... | collective-permute-start | bytes 3145736 | tf_op jit(solution)/shard_map/ppermute | solution.py:374

commit v5 on v4

--- a/solution.py
+++ b/solution.py
@@ -255,7 +255,7 @@
             pltpu.VMEM((NAB - 1, 2 * T, pairs), BF16),
             pltpu.VMEM((NAB - 1, 2, pairs, FREQS * T), BF16),
         ]
-        + [jax.ShapeDtypeStruct((tiles // shares, FREQS, T, T), F32)] * shares,
+        + [pltpu.HBM((tiles // shares, FREQS, T, T), F32)] * shares,
         compiler_params=pltpu.CompilerParams(vmem_limit_bytes=KERNEL_MIB * MIB),
         name="first_products",
     )(picks, got)
@@ -280,7 +280,7 @@
                 pltpu.SemaphoreType.DMA((2,)),
             ],
         ),
-        out_shape=[jax.ShapeDtypeStruct((16, FREQS, T, T), F32)] * 2,
+        out_shape=[pltpu.HBM((16, FREQS, T, T), F32)] * 2,
         compiler_params=pltpu.CompilerParams(vmem_limit_bytes=KERNEL_MIB * MIB),
         cost_estimate=pl.CostEstimate(
             flops=12 * GROUP * FREQS * T * T * left.shape[2], bytes_accessed=4 * MIB, transcendentals=0
@@ -302,6 +302,8 @@
 def add_halves(a, b):
     half = a.shape[0] // 2
     step = 2
+    a = pltpu.with_memory_space_constraint(a, pltpu.HBM)
+    b = pltpu.with_memory_space_constraint(b, pltpu.HBM)
     block = (step,) + a.shape[1:]
     first = pl.BlockSpec(block, lambda i: (i, 0, 0, 0))
     second = pl.BlockSpec(block, lambda i: (i + half // step, 0, 0, 0))
@@ -310,7 +312,7 @@
         grid=(half // step,),
         in_specs=[first, second, first, second],
         out_specs=[first, first],
-        out_shape=[jax.ShapeDtypeStruct((half,) + a.shape[1:], F32)] * 2,
+        out_shape=[pltpu.HBM((half,) + a.shape[1:], F32)] * 2,
         compiler_params=pltpu.CompilerParams(vmem_limit_bytes=KERNEL_MIB * MIB),
         name="add_halves",
     )(a, a, b, b)

time: 219 us -> 219 us (level)
  local copies, waits for them, and re-layouts: 13.3 us -> 3.56 us
  Pallas kernels: 78.3 us -> 85.7 us
    unnamed x27 -> x11, local copies, waits for them, and re-layouts: 11.6 us -> 1.82 us
    pallas_call x2, Pallas kernels: 0.55 us -> 8.38 us  [add_halves(): pl.pallas_call(add_kernel, grid=(half // step,), in_specs=[first, second,...]
  transfers between devices with their start and end apart: 11 -> 11, of which waited for: 2 -> 4; matrix products, arithmetic and copies ran while one was open for 2% -> 1% of each run, Pallas kernels for 17% -> 20%
where the time goes in v5:
time: 219 us; the launch traced here: 218 us
  Pallas kernels  85.7 us (39%)
  waiting for transfers between devices  70.2 us (32%)
  blocking collectives  32.8 us (15%)
  starting transfers between devices  23.4 us (11%)
  local copies, waits for them, and re-layouts  3.56 us (2%)
  other arithmetic  2.43 us (1%)
    all_to_all x1, waiting for transfers between devices, on_device(): got = lax.all_to_all(sent, 'd', split_axis=0, concat_axis=0, tiled=True)  56.6 us
    pallas_call x3, Pallas kernels, more_products(): pl.pallas_call(functools.partial(more_kernel, at, len(fence)), grid_spec=...  36.4 us
    pallas_call x1, Pallas kernels, first_products(): pl.pallas_call(functools.partial(first_kernel, count, blocks, shares), gr...  33.3 us
    all_to_all x1, blocking collectives, on_device(): lax.all_to_all(summed, 'd', split_axis=0, concat_axis=0, tiled=True, axis...  32.8 us
    ppermute x6, waiting for transfers between devices, send(): lax.ppermute(part, 'd', shift(step))  13.6 us
    all_to_all x1, starting transfers between devices, on_device(): got = lax.all_to_all(sent, 'd', split_axis=0, concat_axis=0, tiled=True)  11.9 us
    pallas_call x2, Pallas kernels, add_halves(): pl.pallas_call(add_kernel, grid=(half // step,), in_specs=[first, second,...  8.38 us
    ppermute x6, starting transfers between devices, send(): lax.ppermute(part, 'd', shift(step))  8.1 us
  transfers between devices with their start and end apart: 11, of which 4 were waited for; matrix products, arithmetic and copies ran while one was open for 1% of the time, Pallas kernels for 20%

profile of v5, /device:TPU:1, one launch (start us, length us, event | category | flops | bytes accessed | tf_op | source)
XLA Modules:
  0.0 218.4 jit_solution(8443463979759585099)
XLA Ops:
  0.0 7.7 %columns.1 = f32[128,9,8,128]{3,2,1,0:T(8,128)} custom-call(f32[64,128,128]{2,1,0:T(8,128)} %tiles_ref.1, s32[1,64]{1,0:T(1,128)} %bitcast.31, s32[1,64]{1,0:T(1,128)} %bitcast.32, f32[2,1536]{1,0:T(2,128)} %weights_ref.1), custom_call_target="tpu_custom_call" | custom-call | tf_op jit(solution)/shard_map/columns/pallas_call | solution.py:51
  7.7 11.9 %all-to-all-start = ((f32[128,72,128]{2,1,0:T(8,128)}), f32[128,72,128]{2,1,0:T(8,128)}, u32[]{:S(2)}, u32[]{:S(2)}) async-start(f32[128,72,128]{2,1,0:T(8,128)} %bitcast.30), calls=%async_computation | async-start | bytes 9437184 | tf_op jit(solution)/shard_map/all_to_all | solution.py:360
  19.7 0.0 copy-done.4
  19.7 0.1 copy.7
  19.9 0.1 slice_bitcast_fusion.2
  20.0 0.1 slice_bitcast_fusion
  20.1 0.1 slice_bitcast_fusion.3
  20.1 0.1 slice_bitcast_fusion.1
  20.2 0.1 concatenate.61
  20.3 0.6 gather_fusion
  21.0 0.7 reshape.399.picks
  21.7 56.6 %all-to-all-done.got_ref = f32[128,72,128]{2,1,0:T(8,128)} async-done(((f32[128,72,128]{2,1,0:T(8,128)}), f32[128,72,128]{2,1,0:T(8,128)}, u32[]{:S(2)}, u32[]{:S(2)}) %all-to-all-start) | async-done | bytes 4718624 | tf_op jit(solution)/shard_map/all_to_all | solution.py:360
  78.3 33.3 %first_products.1 = (bf16[19,256,1536]{2,1,0:T(8,128)(2,1)S(1)}, bf16[19,2,1536,256]{3,2,1,0:T(8,128)(2,1)S(1)}, f32[16,2,128,128]{3,2,1,0:T(8,128)}, f32[16,2,128,128]{3,2,1,0:T(8,128)}) custom-call(s32[256]{0:T(256)} %reshape.399.picks, f32[128,72,128]{2,1,0:T(8,128)} %all-to-all-done.got_ref), custom_call_target="tpu_custom_call" | custom-call | tf_op jit(solution)/shard_map/first_products/pallas_call | solution.py:235
  111.6 0.6 collective-permute-start
  112.2 12.1 %more_products.3 = (f32[16,2,128,128]{3,2,1,0:T(8,128)}, f32[16,2,128,128]{3,2,1,0:T(8,128)}) custom-call(s32[256]{0:T(256)} %reshape.399.picks, bf16[19,256,1536]{2,1,0:T(8,128)(2,1)S(1)} %get-tuple-element.29.left, bf16[19,2,1536,256]{3,2,1,0:T(8,128)(2,1)S(1)} %get-tuple-element.30.right), custom_call_target="tpu_custom_call" | custom-call | flops 4831838208 | bytes 4194304 | tf_op jit(solution)/shard_map/more_products/pallas_call | solution.py:270
  124.3 0.0 collective-permute-done.b_low.b_high
  124.3 0.0 copy-start.1
  124.3 0.1 collective-permute-start.1
  124.4 1.3 copy-done.1
  125.7 4.2 %add_halves.2 = (f32[8,2,128,128]{3,2,1,0:T(8,128)}, f32[8,2,128,128]{3,2,1,0:T(8,128)}) custom-call(f32[16,2,128,128]{3,2,1,0:T(8,128)} %get-tuple-element.32.a_low.a_high, f32[16,2,128,128]{3,2,1,0:T(8,128)} %get-tuple-element.32.a_low.a_high, f32[16,2,128,128]{3,2,1,0:T(8,128)} %copy-done.1, f32[16,2,128,128]{3,2,1,0:T(8,128)} %copy-done.1), custom_call_target="tpu_custom_call" | custom-call | tf_op jit(solution)/shard_map/add_halves/pallas_call | solution.py:310
  129.8 0.1 collective-permute-start.2
  130.0 2.6 %collective-permute-start.3 = (f32[8,2,128,128]{3,2,1,0:T(8,128)}, f32[8,2,128,128]{3,2,1,0:T(8,128)S(1)}, u32[]{:S(2)}, u32[]{:S(2)}) collective-permute-start(f32[8,2,128,128]{3,2,1,0:T(8,128)} %get-tuple-element.37.refs_1_), channel_id=1, source_target_pairs={{0,3},{1,0},{2,1},{3,2},{4,100},{5,101},{6,102},{7,103},{8,11},{9,... | collective-permute-start | bytes 3145736 | tf_op jit(solution)/shard_map/ppermute | solution.py:376
  132.5 12.1 %more_products.4 = (f32[16,2,128,128]{3,2,1,0:T(8,128)}, f32[16,2,128,128]{3,2,1,0:T(8,128)}) custom-call(s32[256]{0:T(256)} %reshape.399.picks, bf16[19,256,1536]{2,1,0:T(8,128)(2,1)S(1)} %get-tuple-element.29.left, bf16[19,2,1536,256]{3,2,1,0:T(8,128)(2,1)S(1)} %get-tuple-element.30.right, f32[8,2,128,128]{3,2,1,0:T(8,128)} %get-tuple-element.36.refs_0_, ...), custom_call_target="tpu_custom_call" | custom-call | flops 4831838208 | bytes 4194304 | tf_op jit(solution)/shard_map/more_products/pallas_call | solution.py:270
  144.6 0.6 collective-permute-done.2
  145.2 0.0 collective-permute-done.3
  145.2 0.0 collective-permute-done.1.b_low.b_high
  145.2 1.0 collective-permute-start.4
  146.2 0.4 copy-done
  146.6 4.2 %add_halves.3 = (f32[8,2,128,128]{3,2,1,0:T(8,128)}, f32[8,2,128,128]{3,2,1,0:T(8,128)}) custom-call(f32[16,2,128,128]{3,2,1,0:T(8,128)} %get-tuple-element.31.a_low.a_high, f32[16,2,128,128]{3,2,1,0:T(8,128)} %get-tuple-element.31.a_low.a_high, f32[16,2,128,128]{3,2,1,0:T(8,128)} %copy-done, f32[16,2,128,128]{3,2,1,0:T(8,128)} %copy-done), custom_call_target="tpu_custom_call" | custom-call | tf_op jit(solution)/shard_map/add_halves/pallas_call | solution.py:310
  150.8 0.1 collective-permute-start.5
  150.9 2.6 %collective-permute-start.6 = (f32[8,2,128,128]{3,2,1,0:T(8,128)}, f32[8,2,128,128]{3,2,1,0:T(8,128)S(1)}, u32[]{:S(2)}, u32[]{:S(2)}) collective-permute-start(f32[8,2,128,128]{3,2,1,0:T(8,128)} %get-tuple-element.42.refs_1_), channel_id=1, source_target_pairs={{0,3},{1,0},{2,1},{3,2},{4,100},{5,101},{6,102},{7,103},{8,11},{9,... | collective-permute-start | bytes 3145736 | tf_op jit(solution)/shard_map/ppermute | solution.py:376
  153.5 12.2 %more_products.5 = (f32[16,2,128,128]{3,2,1,0:T(8,128)}, f32[16,2,128,128]{3,2,1,0:T(8,128)}) custom-call(s32[256]{0:T(256)} %reshape.399.picks, bf16[19,256,1536]{2,1,0:T(8,128)(2,1)S(1)} %get-tuple-element.29.left, bf16[19,2,1536,256]{3,2,1,0:T(8,128)(2,1)S(1)} %get-tuple-element.30.right, f32[8,2,128,128]{3,2,1,0:T(8,128)} %get-tuple-element.41.refs_0_, ...), custom_call_target="tpu_custom_call" | custom-call | flops 4831838208 | bytes 4194304 | tf_op jit(solution)/shard_map/more_products/pallas_call | solution.py:270
  165.7 0.5 collective-permute-done.5
  166.2 0.0 collective-permute-done.6
  166.2 0.0 collective-permute-done.4
  166.2 1.7 collective-permute-start.7
  167.9 0.0 copy-done.3
  167.9 0.5 add_add_fusion.1
  168.4 0.2 collective-permute-start.8
  168.7 2.5 %collective-permute-start.9 = (f32[8,2,128,128]{3,2,1,0:T(8,128)S(1)}, f32[8,2,128,128]{3,2,1,0:T(8,128)S(1)}, u32[]{:S(2)}, u32[]{:S(2)}) collective-permute-start(f32[8,2,128,128]{3,2,1,0:T(8,128)S(1)} %get-tuple-element.56), channel_id=1, source_target_pairs={{0,3},{1,0},{2,1},{3,2},{4,100},{5,101},{6,102},{7,103},{8,11},{9,... | collective-permute-start | bytes 3145736 | tf_op jit(solution)/shard_map/ppermute | solution.py:376
  171.2 12.5 %collective-permute-done.8 = f32[8,2,128,128]{3,2,1,0:T(8,128)S(1)} collective-permute-done((f32[8,2,128,128]{3,2,1,0:T(8,128)S(1)}, f32[8,2,128,128]{3,2,1,0:T(8,128)S(1)}, u32[]{:S(2)}, u32[]{:S(2)}) %collective-permute-start.8) | collective-permute-done | bytes 1048608 | tf_op jit(solution)/shard_map/ppermute | solution.py:376
  183.7 0.0 collective-permute-done.9
  183.7 0.0 collective-permute-done.7
  183.7 0.0 copy-done.2
  183.7 0.9 fusion.3
  184.6 0.2 pad_maximum_fusion
  184.8 32.8 %all_to_all.10 = f32[16,2,128,128]{3,2,1,0:T(8,128)S(1)} all-to-all(f32[16,2,128,128]{3,2,1,0:T(8,128)S(1)} %pad_maximum_fusion), channel_id=1, replica_groups={{0,8,16,24,32,40,48,56,64,72,80,88,96,104,112,120},{1,9,17,25,33,41,49,..., dimensions={0} | all-to-all | bytes 4194304 | tf_op jit(solution)/shard_map/all_to_all | solution.py:403
  217.6 0.8 reduce_sum.9
  (10 shorter events, 0.1 us)
Async XLA Ops:
  7.7 12.1 %copy-start.4 = (s32[128,2]{0,1:T(2,128)S(1)}, s32[128,2]{0,1:T(2,128)}, u32[]{:S(2)}) copy-start(s32[128,2]{0,1:T(2,128)} %param.9) | copy-start | bytes 3076
  7.7 70.6 %all-to-all-start = ((f32[128,72,128]{2,1,0:T(8,128)}), f32[128,72,128]{2,1,0:T(8,128)}, u32[]{:S(2)}, u32[]{:S(2)}) async-start(f32[128,72,128]{2,1,0:T(8,128)} %bitcast.30), calls=%async_computation | async-start | bytes 9437184 | tf_op jit(solution)/shard_map/all_to_all | solution.py:360
  111.6 12.7 %collective-permute-start = (f32[16,2,128,128]{3,2,1,0:T(8,128)}, f32[16,2,128,128]{3,2,1,0:T(8,128)S(1)}, u32[]{:S(2)}, u32[]{:S(2)}) collective-permute-start(f32[16,2,128,128]{3,2,1,0:T(8,128)} %get-tuple-element.34), channel_id=1, source_target_pairs={{0,4},{1,5},{2,6},{3,7},{4,0},{5,1},{6,2},{7,3},{8,12},{9,13},{10,... | collective-permute-start | bytes 6291464 | tf_op jit(solution)/shard_map/ppermute | solution.py:373
  124.3 1.4 copy-start.1
  124.3 20.9 %collective-permute-start.1 = (f32[16,2,128,128]{3,2,1,0:T(8,128)}, f32[16,2,128,128]{3,2,1,0:T(8,128)S(1)}, u32[]{:S(2)}, u32[]{:S(2)}) collective-permute-start(f32[16,2,128,128]{3,2,1,0:T(8,128)} %get-tuple-element.39), channel_id=1, source_target_pairs={{0,4},{1,5},{2,6},{3,7},{4,0},{5,1},{6,2},{7,3},{8,12},{9,13},{10,... | collective-permute-start | bytes 6291464 | tf_op jit(solution)/shard_map/ppermute | solution.py:373
  129.8 15.4 %collective-permute-start.2 = (f32[8,2,128,128]{3,2,1,0:T(8,128)}, f32[8,2,128,128]{3,2,1,0:T(8,128)S(1)}, u32[]{:S(2)}, u32[]{:S(2)}) collective-permute-start(f32[8,2,128,128]{3,2,1,0:T(8,128)} %get-tuple-element.36.refs_0_), channel_id=1, source_target_pairs={{0,1},{1,2},{2,3},{3,0},{4,36},{5,37},{6,38},{7,39},{8,9},{9,10},{... | collective-permute-start | bytes 3145736 | tf_op jit(solution)/shard_map/ppermute | solution.py:376
  130.0 15.2 %collective-permute-start.3 = (f32[8,2,128,128]{3,2,1,0:T(8,128)}, f32[8,2,128,128]{3,2,1,0:T(8,128)S(1)}, u32[]{:S(2)}, u32[]{:S(2)}) collective-permute-start(f32[8,2,128,128]{3,2,1,0:T(8,128)} %get-tuple-element.37.refs_1_), channel_id=1, source_target_pairs={{0,3},{1,0},{2,1},{3,2},{4,100},{5,101},{6,102},{7,103},{8,11},{9,... | collective-permute-start | bytes 3145736 | tf_op jit(solution)/shard_map/ppermute | solution.py:376
  145.2 1.4 copy-start
  145.2 21.0 %collective-permute-start.4 = (f32[16,2,128,128]{3,2,1,0:T(8,128)}, f32[16,2,128,128]{3,2,1,0:T(8,128)S(1)}, u32[]{:S(2)}, u32[]{:S(2)}) collective-permute-start(f32[16,2,128,128]{3,2,1,0:T(8,128)} %get-tuple-element.45), channel_id=1, source_target_pairs={{0,4},{1,5},{2,6},{3,7},{4,0},{5,1},{6,2},{7,3},{8,12},{9,13},{10,... | collective-permute-start | bytes 6291464 | tf_op jit(solution)/shard_map/ppermute | solution.py:373
  150.8 15.4 %collective-permute-start.5 = (f32[8,2,128,128]{3,2,1,0:T(8,128)}, f32[8,2,128,128]{3,2,1,0:T(8,128)S(1)}, u32[]{:S(2)}, u32[]{:S(2)}) collective-permute-start(f32[8,2,128,128]{3,2,1,0:T(8,128)} %get-tuple-element.41.refs_0_), channel_id=1, source_target_pairs={{0,1},{1,2},{2,3},{3,0},{4,36},{5,37},{6,38},{7,39},{8,9},{9,10},{... | collective-permute-start | bytes 3145736 | tf_op jit(solution)/shard_map/ppermute | solution.py:376
  150.9 17.0 %copy-start.3 = (f32[16,2,128,128]{3,2,1,0:T(8,128)S(1)}, f32[16,2,128,128]{3,2,1,0:T(8,128)}, u32[]{:S(2)}) copy-start(f32[16,2,128,128]{3,2,1,0:T(8,128)} %get-tuple-element.47) | copy-start | bytes 6291460
  150.9 15.3 %collective-permute-start.6 = (f32[8,2,128,128]{3,2,1,0:T(8,128)}, f32[8,2,128,128]{3,2,1,0:T(8,128)S(1)}, u32[]{:S(2)}, u32[]{:S(2)}) collective-permute-start(f32[8,2,128,128]{3,2,1,0:T(8,128)} %get-tuple-element.42.refs_1_), channel_id=1, source_target_pairs={{0,3},{1,0},{2,1},{3,2},{4,100},{5,101},{6,102},{7,103},{8,11},{9,... | collective-permute-start | bytes 3145736 | tf_op jit(solution)/shard_map/ppermute | solution.py:376
  166.2 17.5 %collective-permute-start.7 = (f32[16,2,128,128]{3,2,1,0:T(8,128)}, f32[16,2,128,128]{3,2,1,0:T(8,128)S(1)}, u32[]{:S(2)}, u32[]{:S(2)}) collective-permute-start(f32[16,2,128,128]{3,2,1,0:T(8,128)} %get-tuple-element.46), channel_id=1, source_target_pairs={{0,4},{1,5},{2,6},{3,7},{4,0},{5,1},{6,2},{7,3},{8,12},{9,13},{10,... | collective-permute-start | bytes 6291464 | tf_op jit(solution)/shard_map/ppermute | solution.py:373
  167.9 15.8 %copy-start.2 = (f32[16,2,128,128]{3,2,1,0:T(8,128)S(1)}, f32[16,2,128,128]{3,2,1,0:T(8,128)}, u32[]{:S(2)}) copy-start(f32[16,2,128,128]{3,2,1,0:T(8,128)} %get-tuple-element.43) | copy-start | bytes 6291460
  168.4 15.2 %collective-permute-start.8 = (f32[8,2,128,128]{3,2,1,0:T(8,128)S(1)}, f32[8,2,128,128]{3,2,1,0:T(8,128)S(1)}, u32[]{:S(2)}, u32[]{:S(2)}) collective-permute-start(f32[8,2,128,128]{3,2,1,0:T(8,128)S(1)} %get-tuple-element.55), channel_id=1, source_target_pairs={{0,1},{1,2},{2,3},{3,0},{4,36},{5,37},{6,38},{7,39},{8,9},{9,10},{... | collective-permute-start | bytes 3145736 | tf_op jit(solution)/shard_map/ppermute | solution.py:376
  168.7 15.0 %collective-permute-start.9 = (f32[8,2,128,128]{3,2,1,0:T(8,128)S(1)}, f32[8,2,128,128]{3,2,1,0:T(8,128)S(1)}, u32[]{:S(2)}, u32[]{:S(2)}) collective-permute-start(f32[8,2,128,128]{3,2,1,0:T(8,128)S(1)} %get-tuple-element.56), channel_id=1, source_target_pairs={{0,3},{1,0},{2,1},{3,2},{4,100},{5,101},{6,102},{7,103},{8,11},{9,... | collective-permute-start | bytes 3145736 | tf_op jit(solution)/shard_map/ppermute | solution.py:376

commit v6 on v5

--- a/solution.py
+++ b/solution.py
@@ -65,10 +65,11 @@
 
 def multiply(begin, picks, left, right, stage, outs, out_sems):
     share = outs[0].shape[0]
+    size = stage.shape[1]
 
     def copies(g):
         buffer = lax.rem(g, 2)
-        at = pl.ds(lax.rem(g, share // GROUP) * GROUP, GROUP)
+        at = pl.ds(lax.rem(g, share // size) * size, size)
         return [pltpu.make_async_copy(stage.at[buffer], out.at[at], out_sems.at[buffer]) for out in outs]
 
     def group(g, carry):
@@ -78,9 +79,9 @@
         def _():
             copies(g)[0].wait()
 
-        for k in range(GROUP):
-            p = picks[2 * (begin + g * GROUP + k)]
-            q = picks[2 * (begin + g * GROUP + k) + 1] - 1
+        for k in range(size):
+            p = picks[2 * (begin + g * size + k)]
+            q = picks[2 * (begin + g * size + k) + 1] - 1
             both = jnp.dot(left[p], right[q, 0], preferred_element_type=F32)
             small = jnp.dot(left[p, 0:T, :], right[q, 1], preferred_element_type=F32)
             result = both[0:T] + (both[T:] + small)
@@ -88,13 +89,13 @@
                 stage[buffer, k, f] = result[:, f * T : (f + 1) * T]
         for i, copy in enumerate(copies(g)):
 
-            @pl.when(g // (share // GROUP) == i)
+            @pl.when(g // (share // size) == i)
             def _():
                 copy.start()
 
         return carry
 
-    lax.fori_loop(0, len(outs) * share // GROUP, group, 0)
+    lax.fori_loop(0, len(outs) * share // size, group, 0)
     for g in range(2):
         copies(g)[0].wait()
 
@@ -276,7 +277,7 @@
             + [pl.BlockSpec(memory_space=pl.ANY)] * len(fence),
             out_specs=[pl.BlockSpec(memory_space=pl.ANY)] * 2,
             scratch_shapes=[
-                pltpu.VMEM((2, GROUP, FREQS, T, T), F32),
+                pltpu.VMEM((2, 16, FREQS, T, T), F32),
                 pltpu.SemaphoreType.DMA((2,)),
             ],
         ),
@@ -301,7 +302,7 @@
 
 def add_halves(a, b):
     half = a.shape[0] // 2
-    step = 2
+    step = 4
     a = pltpu.with_memory_space_constraint(a, pltpu.HBM)
     b = pltpu.with_memory_space_constraint(b, pltpu.HBM)
     block = (step,) + a.shape[1:]

time: 219 us -> 217 us (level)
  no operation moved by 1% of the time
where the time goes in v6:
time: 217 us
  Pallas kernels  83.9 us (39%)
  waiting for transfers between devices  70.2 us (32%)
  blocking collectives  32.8 us (15%)
  starting transfers between devices  23.6 us (11%)
  local copies, waits for them, and re-layouts  3.38 us (2%)
  other arithmetic  2.43 us (1%)
    all_to_all x1, waiting for transfers between devices, on_device(): got = lax.all_to_all(sent, 'd', split_axis=0, concat_axis=0, tiled=True)  56.6 us
    pallas_call x3, Pallas kernels, more_products(): pl.pallas_call(functools.partial(more_kernel, at, len(fence)), grid_spec=...  36.4 us
    pallas_call x1, Pallas kernels, first_products(): pl.pallas_call(functools.partial(first_kernel, count, blocks, shares), gr...  33.3 us
    all_to_all x1, blocking collectives, on_device(): lax.all_to_all(summed, 'd', split_axis=0, concat_axis=0, tiled=True, axis...  32.8 us
    ppermute x6, waiting for transfers between devices, send(): lax.ppermute(part, 'd', shift(step))  13.5 us
    all_to_all x1, starting transfers between devices, on_device(): got = lax.all_to_all(sent, 'd', split_axis=0, concat_axis=0, tiled=True)  11.9 us
    ppermute x6, starting transfers between devices, send(): lax.ppermute(part, 'd', shift(step))  8.1 us
    pallas_call x1, Pallas kernels, by_column(): pl.pallas_call(functools.partial(columns_kernel, groups, blocks, devices)...  7.66 us
  transfers between devices with their start and end apart: 11, of which 4 were waited for; matrix products, arithmetic and copies ran while one was open for 1% of the time, Pallas kernels for 20%

profile of v6, /device:TPU:1, one launch (start us, length us, event | category | flops | bytes accessed | tf_op | source)
XLA Modules:
  0.0 216.6 jit_solution(8183290992437036681)
XLA Ops:
  0.0 7.7 %columns.1 = f32[128,9,8,128]{3,2,1,0:T(8,128)} custom-call(f32[64,128,128]{2,1,0:T(8,128)} %tiles_ref.1, s32[1,64]{1,0:T(1,128)} %bitcast.31, s32[1,64]{1,0:T(1,128)} %bitcast.32, f32[2,1536]{1,0:T(2,128)} %weights_ref.1), custom_call_target="tpu_custom_call" | custom-call | tf_op jit(solution)/shard_map/columns/pallas_call | solution.py:51
  7.7 11.9 %all-to-all-start = ((f32[128,72,128]{2,1,0:T(8,128)}), f32[128,72,128]{2,1,0:T(8,128)}, u32[]{:S(2)}, u32[]{:S(2)}) async-start(f32[128,72,128]{2,1,0:T(8,128)} %bitcast.30), calls=%async_computation | async-start | bytes 9437184 | tf_op jit(solution)/shard_map/all_to_all | solution.py:361
  19.7 0.0 copy-done.4
  19.7 0.1 copy.7
  19.9 0.1 slice_bitcast_fusion.2
  20.0 0.1 slice_bitcast_fusion
  20.1 0.1 slice_bitcast_fusion.3
  20.1 0.1 slice_bitcast_fusion.1
  20.2 0.1 concatenate.61
  20.3 0.6 gather_fusion
  21.0 0.7 reshape.399.picks
  21.7 56.6 %all-to-all-done.got_ref = f32[128,72,128]{2,1,0:T(8,128)} async-done(((f32[128,72,128]{2,1,0:T(8,128)}), f32[128,72,128]{2,1,0:T(8,128)}, u32[]{:S(2)}, u32[]{:S(2)}) %all-to-all-start) | async-done | bytes 4718624 | tf_op jit(solution)/shard_map/all_to_all | solution.py:361
  78.3 33.3 %first_products.1 = (bf16[19,256,1536]{2,1,0:T(8,128)(2,1)S(1)}, bf16[19,2,1536,256]{3,2,1,0:T(8,128)(2,1)S(1)}, f32[16,2,128,128]{3,2,1,0:T(8,128)}, f32[16,2,128,128]{3,2,1,0:T(8,128)}) custom-call(s32[256]{0:T(256)} %reshape.399.picks, f32[128,72,128]{2,1,0:T(8,128)} %all-to-all-done.got_ref), custom_call_target="tpu_custom_call" | custom-call | tf_op jit(solution)/shard_map/first_products/pallas_call | solution.py:236
  111.6 0.6 collective-permute-start
  112.2 12.1 %more_products.3 = (f32[16,2,128,128]{3,2,1,0:T(8,128)}, f32[16,2,128,128]{3,2,1,0:T(8,128)}) custom-call(s32[256]{0:T(256)} %reshape.399.picks, bf16[19,256,1536]{2,1,0:T(8,128)(2,1)S(1)} %get-tuple-element.29.left, bf16[19,2,1536,256]{3,2,1,0:T(8,128)(2,1)S(1)} %get-tuple-element.30.right), custom_call_target="tpu_custom_call" | custom-call | flops 4831838208 | bytes 4194304 | tf_op jit(solution)/shard_map/more_products/pallas_call | solution.py:271
  124.3 0.0 collective-permute-done.b_low.b_high
  124.4 0.0 copy-start.1
  124.4 0.3 collective-permute-start.1
  124.6 1.1 copy-done.1
  125.7 3.3 %add_halves.2 = (f32[8,2,128,128]{3,2,1,0:T(8,128)}, f32[8,2,128,128]{3,2,1,0:T(8,128)}) custom-call(f32[16,2,128,128]{3,2,1,0:T(8,128)} %get-tuple-element.32.a_low.a_high, f32[16,2,128,128]{3,2,1,0:T(8,128)} %get-tuple-element.32.a_low.a_high, f32[16,2,128,128]{3,2,1,0:T(8,128)} %copy-done.1, f32[16,2,128,128]{3,2,1,0:T(8,128)} %copy-done.1), custom_call_target="tpu_custom_call" | custom-call | tf_op jit(solution)/shard_map/add_halves/pallas_call | solution.py:311
  129.0 0.1 collective-permute-start.2
  129.1 2.5 %collective-permute-start.3 = (f32[8,2,128,128]{3,2,1,0:T(8,128)}, f32[8,2,128,128]{3,2,1,0:T(8,128)S(1)}, u32[]{:S(2)}, u32[]{:S(2)}) collective-permute-start(f32[8,2,128,128]{3,2,1,0:T(8,128)} %get-tuple-element.37.refs_1_), channel_id=1, source_target_pairs={{0,3},{1,0},{2,1},{3,2},{4,100},{5,101},{6,102},{7,103},{8,11},{9,... | collective-permute-start | bytes 3145736 | tf_op jit(solution)/shard_map/ppermute | solution.py:377
  131.7 12.1 %more_products.4 = (f32[16,2,128,128]{3,2,1,0:T(8,128)}, f32[16,2,128,128]{3,2,1,0:T(8,128)}) custom-call(s32[256]{0:T(256)} %reshape.399.picks, bf16[19,256,1536]{2,1,0:T(8,128)(2,1)S(1)} %get-tuple-element.29.left, bf16[19,2,1536,256]{3,2,1,0:T(8,128)(2,1)S(1)} %get-tuple-element.30.right, f32[8,2,128,128]{3,2,1,0:T(8,128)} %get-tuple-element.36.refs_0_, ...), custom_call_target="tpu_custom_call" | custom-call | flops 4831838208 | bytes 4194304 | tf_op jit(solution)/shard_map/more_products/pallas_call | solution.py:271
  143.8 0.5 collective-permute-done.2
  144.3 0.0 collective-permute-done.3
  144.3 0.0 collective-permute-done.1.b_low.b_high
  144.4 1.0 collective-permute-start.4
  145.3 0.4 copy-done
  145.7 3.3 %add_halves.3 = (f32[8,2,128,128]{3,2,1,0:T(8,128)}, f32[8,2,128,128]{3,2,1,0:T(8,128)}) custom-call(f32[16,2,128,128]{3,2,1,0:T(8,128)} %get-tuple-element.31.a_low.a_high, f32[16,2,128,128]{3,2,1,0:T(8,128)} %get-tuple-element.31.a_low.a_high, f32[16,2,128,128]{3,2,1,0:T(8,128)} %copy-done, f32[16,2,128,128]{3,2,1,0:T(8,128)} %copy-done), custom_call_target="tpu_custom_call" | custom-call | tf_op jit(solution)/shard_map/add_halves/pallas_call | solution.py:311
  149.0 0.1 collective-permute-start.5
  149.1 2.6 %collective-permute-start.6 = (f32[8,2,128,128]{3,2,1,0:T(8,128)}, f32[8,2,128,128]{3,2,1,0:T(8,128)S(1)}, u32[]{:S(2)}, u32[]{:S(2)}) collective-permute-start(f32[8,2,128,128]{3,2,1,0:T(8,128)} %get-tuple-element.42.refs_1_), channel_id=1, source_target_pairs={{0,3},{1,0},{2,1},{3,2},{4,100},{5,101},{6,102},{7,103},{8,11},{9,... | collective-permute-start | bytes 3145736 | tf_op jit(solution)/shard_map/ppermute | solution.py:377
  151.7 12.2 %more_products.5 = (f32[16,2,128,128]{3,2,1,0:T(8,128)}, f32[16,2,128,128]{3,2,1,0:T(8,128)}) custom-call(s32[256]{0:T(256)} %reshape.399.picks, bf16[19,256,1536]{2,1,0:T(8,128)(2,1)S(1)} %get-tuple-element.29.left, bf16[19,2,1536,256]{3,2,1,0:T(8,128)(2,1)S(1)} %get-tuple-element.30.right, f32[8,2,128,128]{3,2,1,0:T(8,128)} %get-tuple-element.41.refs_0_, ...), custom_call_target="tpu_custom_call" | custom-call | flops 4831838208 | bytes 4194304 | tf_op jit(solution)/shard_map/more_products/pallas_call | solution.py:271
  163.9 0.5 collective-permute-done.5
  164.4 0.0 collective-permute-done.6
  164.4 0.0 collective-permute-done.4
  164.4 1.7 collective-permute-start.7
  166.1 0.0 copy-done.3
  166.1 0.5 add_add_fusion.1
  166.7 0.2 collective-permute-start.8
  166.9 2.5 %collective-permute-start.9 = (f32[8,2,128,128]{3,2,1,0:T(8,128)S(1)}, f32[8,2,128,128]{3,2,1,0:T(8,128)S(1)}, u32[]{:S(2)}, u32[]{:S(2)}) collective-permute-start(f32[8,2,128,128]{3,2,1,0:T(8,128)S(1)} %get-tuple-element.56), channel_id=1, source_target_pairs={{0,3},{1,0},{2,1},{3,2},{4,100},{5,101},{6,102},{7,103},{8,11},{9,... | collective-permute-start | bytes 3145736 | tf_op jit(solution)/shard_map/ppermute | solution.py:377
  169.4 12.5 %collective-permute-done.8 = f32[8,2,128,128]{3,2,1,0:T(8,128)S(1)} collective-permute-done((f32[8,2,128,128]{3,2,1,0:T(8,128)S(1)}, f32[8,2,128,128]{3,2,1,0:T(8,128)S(1)}, u32[]{:S(2)}, u32[]{:S(2)}) %collective-permute-start.8) | collective-permute-done | bytes 1048608 | tf_op jit(solution)/shard_map/ppermute | solution.py:377
  181.9 0.0 collective-permute-done.9
  181.9 0.0 collective-permute-done.7
  181.9 0.0 copy-done.2
  181.9 0.9 fusion.3
  182.8 0.2 pad_maximum_fusion
  183.0 32.8 %all_to_all.10 = f32[16,2,128,128]{3,2,1,0:T(8,128)S(1)} all-to-all(f32[16,2,128,128]{3,2,1,0:T(8,128)S(1)} %pad_maximum_fusion), channel_id=1, replica_groups={{0,8,16,24,32,40,48,56,64,72,80,88,96,104,112,120},{1,9,17,25,33,41,49,..., dimensions={0} | all-to-all | bytes 4194304 | tf_op jit(solution)/shard_map/all_to_all | solution.py:404
  215.8 0.8 reduce_sum.9
  (10 shorter events, 0.1 us)
Async XLA Ops:
  7.7 12.1 %copy-start.4 = (s32[128,2]{0,1:T(2,128)S(1)}, s32[128,2]{0,1:T(2,128)}, u32[]{:S(2)}) copy-start(s32[128,2]{0,1:T(2,128)} %param.9) | copy-start | bytes 3076
  7.7 70.6 %all-to-all-start = ((f32[128,72,128]{2,1,0:T(8,128)}), f32[128,72,128]{2,1,0:T(8,128)}, u32[]{:S(2)}, u32[]{:S(2)}) async-start(f32[128,72,128]{2,1,0:T(8,128)} %bitcast.30), calls=%async_computation | async-start | bytes 9437184 | tf_op jit(solution)/shard_map/all_to_all | solution.py:361
  111.6 12.8 %collective-permute-start = (f32[16,2,128,128]{3,2,1,0:T(8,128)}, f32[16,2,128,128]{3,2,1,0:T(8,128)S(1)}, u32[]{:S(2)}, u32[]{:S(2)}) collective-permute-start(f32[16,2,128,128]{3,2,1,0:T(8,128)} %get-tuple-element.34), channel_id=1, source_target_pairs={{0,4},{1,5},{2,6},{3,7},{4,0},{5,1},{6,2},{7,3},{8,12},{9,13},{10,... | collective-permute-start | bytes 6291464 | tf_op jit(solution)/shard_map/ppermute | solution.py:374
  124.4 1.4 copy-start.1
  124.4 20.0 %collective-permute-start.1 = (f32[16,2,128,128]{3,2,1,0:T(8,128)}, f32[16,2,128,128]{3,2,1,0:T(8,128)S(1)}, u32[]{:S(2)}, u32[]{:S(2)}) collective-permute-start(f32[16,2,128,128]{3,2,1,0:T(8,128)} %get-tuple-element.39), channel_id=1, source_target_pairs={{0,4},{1,5},{2,6},{3,7},{4,0},{5,1},{6,2},{7,3},{8,12},{9,13},{10,... | collective-permute-start | bytes 6291464 | tf_op jit(solution)/shard_map/ppermute | solution.py:374
  129.0 15.4 %collective-permute-start.2 = (f32[8,2,128,128]{3,2,1,0:T(8,128)}, f32[8,2,128,128]{3,2,1,0:T(8,128)S(1)}, u32[]{:S(2)}, u32[]{:S(2)}) collective-permute-start(f32[8,2,128,128]{3,2,1,0:T(8,128)} %get-tuple-element.36.refs_0_), channel_id=1, source_target_pairs={{0,1},{1,2},{2,3},{3,0},{4,36},{5,37},{6,38},{7,39},{8,9},{9,10},{... | collective-permute-start | bytes 3145736 | tf_op jit(solution)/shard_map/ppermute | solution.py:377
  129.1 15.2 %collective-permute-start.3 = (f32[8,2,128,128]{3,2,1,0:T(8,128)}, f32[8,2,128,128]{3,2,1,0:T(8,128)S(1)}, u32[]{:S(2)}, u32[]{:S(2)}) collective-permute-start(f32[8,2,128,128]{3,2,1,0:T(8,128)} %get-tuple-element.37.refs_1_), channel_id=1, source_target_pairs={{0,3},{1,0},{2,1},{3,2},{4,100},{5,101},{6,102},{7,103},{8,11},{9,... | collective-permute-start | bytes 3145736 | tf_op jit(solution)/shard_map/ppermute | solution.py:377
  144.4 1.4 copy-start
  144.4 20.0 %collective-permute-start.4 = (f32[16,2,128,128]{3,2,1,0:T(8,128)}, f32[16,2,128,128]{3,2,1,0:T(8,128)S(1)}, u32[]{:S(2)}, u32[]{:S(2)}) collective-permute-start(f32[16,2,128,128]{3,2,1,0:T(8,128)} %get-tuple-element.45), channel_id=1, source_target_pairs={{0,4},{1,5},{2,6},{3,7},{4,0},{5,1},{6,2},{7,3},{8,12},{9,13},{10,... | collective-permute-start | bytes 6291464 | tf_op jit(solution)/shard_map/ppermute | solution.py:374
  149.0 15.4 %collective-permute-start.5 = (f32[8,2,128,128]{3,2,1,0:T(8,128)}, f32[8,2,128,128]{3,2,1,0:T(8,128)S(1)}, u32[]{:S(2)}, u32[]{:S(2)}) collective-permute-start(f32[8,2,128,128]{3,2,1,0:T(8,128)} %get-tuple-element.41.refs_0_), channel_id=1, source_target_pairs={{0,1},{1,2},{2,3},{3,0},{4,36},{5,37},{6,38},{7,39},{8,9},{9,10},{... | collective-permute-start | bytes 3145736 | tf_op jit(solution)/shard_map/ppermute | solution.py:377
  149.1 17.0 %copy-start.3 = (f32[16,2,128,128]{3,2,1,0:T(8,128)S(1)}, f32[16,2,128,128]{3,2,1,0:T(8,128)}, u32[]{:S(2)}) copy-start(f32[16,2,128,128]{3,2,1,0:T(8,128)} %get-tuple-element.47) | copy-start | bytes 6291460
  149.1 15.3 %collective-permute-start.6 = (f32[8,2,128,128]{3,2,1,0:T(8,128)}, f32[8,2,128,128]{3,2,1,0:T(8,128)S(1)}, u32[]{:S(2)}, u32[]{:S(2)}) collective-permute-start(f32[8,2,128,128]{3,2,1,0:T(8,128)} %get-tuple-element.42.refs_1_), channel_id=1, source_target_pairs={{0,3},{1,0},{2,1},{3,2},{4,100},{5,101},{6,102},{7,103},{8,11},{9,... | collective-permute-start | bytes 3145736 | tf_op jit(solution)/shard_map/ppermute | solution.py:377
  164.4 17.5 %collective-permute-start.7 = (f32[16,2,128,128]{3,2,1,0:T(8,128)}, f32[16,2,128,128]{3,2,1,0:T(8,128)S(1)}, u32[]{:S(2)}, u32[]{:S(2)}) collective-permute-start(f32[16,2,128,128]{3,2,1,0:T(8,128)} %get-tuple-element.46), channel_id=1, source_target_pairs={{0,4},{1,5},{2,6},{3,7},{4,0},{5,1},{6,2},{7,3},{8,12},{9,13},{10,... | collective-permute-start | bytes 6291464 | tf_op jit(solution)/shard_map/ppermute | solution.py:374
  166.1 15.8 %copy-start.2 = (f32[16,2,128,128]{3,2,1,0:T(8,128)S(1)}, f32[16,2,128,128]{3,2,1,0:T(8,128)}, u32[]{:S(2)}) copy-start(f32[16,2,128,128]{3,2,1,0:T(8,128)} %get-tuple-element.43) | copy-start | bytes 6291460
  166.7 15.2 %collective-permute-start.8 = (f32[8,2,128,128]{3,2,1,0:T(8,128)S(1)}, f32[8,2,128,128]{3,2,1,0:T(8,128)S(1)}, u32[]{:S(2)}, u32[]{:S(2)}) collective-permute-start(f32[8,2,128,128]{3,2,1,0:T(8,128)S(1)} %get-tuple-element.55), channel_id=1, source_target_pairs={{0,1},{1,2},{2,3},{3,0},{4,36},{5,37},{6,38},{7,39},{8,9},{9,10},{... | collective-permute-start | bytes 3145736 | tf_op jit(solution)/shard_map/ppermute | solution.py:377
  166.9 15.0 %collective-permute-start.9 = (f32[8,2,128,128]{3,2,1,0:T(8,128)S(1)}, f32[8,2,128,128]{3,2,1,0:T(8,128)S(1)}, u32[]{:S(2)}, u32[]{:S(2)}) collective-permute-start(f32[8,2,128,128]{3,2,1,0:T(8,128)S(1)} %get-tuple-element.56), channel_id=1, source_target_pairs={{0,3},{1,0},{2,1},{3,2},{4,100},{5,101},{6,102},{7,103},{8,11},{9,... | collective-permute-start | bytes 3145736 | tf_op jit(solution)/shard_map/ppermute | solution.py:377
